TPU v7x, 512 devices: a whole 4x4x16 slice. The times are simulated.
512 devices in a mesh: rollout: 16 (over z), ctx: 32 (over y, x, core).
Axes of the slice: x: 4, y: 4, z: 16, core: 2. Of those that a mesh axis runs over, the one named last changes fastest.
Arguments:
- queries: bfloat16 [16, 4096, 4096], P('rollout', 'ctx'), may hold values from -6 to 6
- keys_values: bfloat16 [16, 2, 4096, 1024], P('rollout', None, 'ctx'), may hold values from -6 to 6
- image_rows: bfloat16 [16, 256, 6144], P('rollout', 'ctx'), may hold values from -6 to 6
- cotangent: bfloat16 [16, 4096, 4096], P('rollout', 'ctx'), may hold values from -96 to 96
- seq_image: int32 [16], replicated, may hold values from 0 to 15, as said below
- vis_start: int32 [16], P('rollout'), may hold values from 1 to 63
- comp_lengths: int32 [16, 16], P('rollout'), may hold values from 1 to 314, 3776 in all within a row
Outputs:
- grad_queries: bfloat16 [16, 4096, 4096], P('rollout', 'ctx')
- grad_keys_values: bfloat16 [16, 2, 4096, 1024], P('rollout', None, 'ctx')
- grad_image: bfloat16 [16, 256, 6144], P('rollout', 'ctx')
Inputs may be any that keep to these rules, and one draw needn't show every extreme that they name: `seq_image`: each image belongs to exactly one group. The image's rows take positions vis_start to vis_start + 255 of the group's sequence. `comp_lengths`: each group's lengths sum to 3776.
All inputs are finite; a program needn't handle non-finite values.
Results may differ from a plain program's by a relative error of at most 0.0068.
Values may be sent and summed in bfloat16 or wider, within the bound.
A program may use at most 128 MiB of HBM per device.

v0:
```python
import math

import jax
import jax.numpy as jnp
from jax import lax
from jax.sharding import PartitionSpec as P

HEADS = 32
KV_HEADS = 8
HEAD_DIM = 128
VIS = 256
PROMPT = 64


neg_large = -1e30


def contract_last(left, right):
    return lax.dot_general(
        left, right, (((1,), (1,)), ((), ())), preferred_element_type=jnp.float32
    )


def contract_first(left, right):
    return lax.dot_general(
        left, right, (((0,), (0,)), ((), ())), preferred_element_type=jnp.float32
    )


def head_layout(q_rows, kv_rows, head_ratio):
    row_count = q_rows.shape[0]
    q_part = q_rows.reshape(1, row_count, HEADS, HEAD_DIM)
    kv_part = jnp.repeat(kv_rows.reshape(2, row_count, KV_HEADS, HEAD_DIM), head_ratio, axis=2)
    return jnp.concatenate([q_part, kv_part], axis=0)


def fold_heads(block, head_ratio):
    row_count = block.shape[1]
    q_part = block[0].reshape(row_count, HEADS * HEAD_DIM).astype(jnp.bfloat16)
    kv_part = jnp.sum(
        block[1:].reshape(2, row_count, KV_HEADS, head_ratio, HEAD_DIM), axis=3, dtype=jnp.float32
    )
    return (q_part, kv_part.astype(jnp.bfloat16).reshape(2, row_count, KV_HEADS * HEAD_DIM))


def attend(q_head, k_head, v_head, d_head, segment_ids, segment_begin):
    seq_len, head_dim = q_head.shape
    q_block = min(512, seq_len)
    k_block = min(128, seq_len)
    score_scale = 1.0 / math.sqrt(head_dim)
    prefix_len = VIS + PROMPT
    key_blocks = seq_len // k_block
    prefix_blocks = min(-(-prefix_len // k_block), key_blocks)
    column_ids = jnp.arange(k_block, dtype=jnp.int32)
    row_ids = jnp.arange(q_block, dtype=jnp.int32)

    def key_rows(key_index):
        k_begin = key_index * k_block
        k_rows = lax.dynamic_slice_in_dim(k_head, k_begin, k_block, 0)
        v_rows = lax.dynamic_slice_in_dim(v_head, k_begin, k_block, 0)
        seg_cols = lax.dynamic_slice_in_dim(segment_ids, k_begin, k_block, 0)
        return (k_rows, v_rows, seg_cols, k_begin)

    def query_step(block_index, loop_carry):
        dq_out, dk_acc, dv_acc, score_store = loop_carry
        q_begin = block_index * q_block
        q_rows = lax.dynamic_slice_in_dim(q_head, q_begin, q_block, 0)
        d_rows = lax.dynamic_slice_in_dim(d_head, q_begin, q_block, 0)
        seg_rows = lax.dynamic_slice_in_dim(segment_ids, q_begin, q_block, 0)
        positions = q_begin + row_ids
        first_seg = seg_rows[0]
        first_key = jnp.where(first_seg == 0, 0, segment_begin[jnp.maximum(first_seg - 1, 0)])
        upper = (q_begin + q_block - 1) // k_block + 1
        lower = jnp.maximum(first_key // k_block, prefix_blocks)
        prefix_upper = jnp.minimum(prefix_blocks, upper)

        def stats_step(key_index, running):
            row_top, row_total, row_mix, stored = running
            k_rows, v_rows, seg_cols, k_begin = key_rows(key_index)
            visible = ((k_begin + column_ids)[None, :] <= positions[:, None]) & (
                (seg_cols[None, :] == 0) | (seg_cols[None, :] == seg_rows[:, None])
            )
            scores = jnp.where(visible, contract_last(q_rows, k_rows) * score_scale, neg_large)
            d_weights = contract_last(d_rows, v_rows)
            new_top = jnp.maximum(row_top, jnp.max(scores, axis=1))
            shrink = jnp.exp(row_top - new_top)
            exp_terms = jnp.where(visible, jnp.exp(scores - new_top[:, None]), 0.0)
            stored = lax.dynamic_update_index_in_dim(stored, scores, key_index, 0)
            return (
                new_top,
                row_total * shrink + jnp.sum(exp_terms, axis=1),
                row_mix * shrink + jnp.sum(exp_terms * d_weights, axis=1),
                stored,
            )

        running = (
            jnp.full((q_block,), neg_large, jnp.float32),
            jnp.zeros((q_block,), jnp.float32),
            jnp.zeros((q_block,), jnp.float32),
            score_store,
        )
        running = lax.fori_loop(0, prefix_upper, stats_step, running)
        running = lax.fori_loop(lower, upper, stats_step, running)
        row_top, row_total, row_mix, score_store = running
        row_delta = row_mix / row_total

        def grad_step(key_index, sums):
            dq_acc, dk_sums, dv_sums = sums
            k_rows, v_rows, seg_cols, k_begin = key_rows(key_index)
            scores = lax.dynamic_index_in_dim(score_store, key_index, 0, keepdims=False)
            weights = jnp.exp(scores - row_top[:, None]) / row_total[:, None]
            d_weights = contract_last(d_rows, v_rows)
            d_scores = (weights * (d_weights - row_delta[:, None])).astype(jnp.bfloat16)
            dq_acc = dq_acc + jnp.dot(d_scores, k_rows, preferred_element_type=jnp.float32)
            dk_part = contract_first(d_scores, q_rows)
            dv_part = contract_first(weights.astype(jnp.bfloat16), d_rows)
            dk_sums = lax.dynamic_update_slice_in_dim(
                dk_sums,
                lax.dynamic_slice_in_dim(dk_sums, k_begin, k_block, 0) + dk_part,
                k_begin,
                0,
            )
            dv_sums = lax.dynamic_update_slice_in_dim(
                dv_sums,
                lax.dynamic_slice_in_dim(dv_sums, k_begin, k_block, 0) + dv_part,
                k_begin,
                0,
            )
            return (dq_acc, dk_sums, dv_sums)

        sums = (jnp.zeros((q_block, head_dim), jnp.float32), dk_acc, dv_acc)
        sums = lax.fori_loop(0, prefix_upper, grad_step, sums)
        dq_acc, dk_acc, dv_acc = lax.fori_loop(lower, upper, grad_step, sums)
        dq_out = lax.dynamic_update_slice_in_dim(dq_out, dq_acc * score_scale, q_begin, 0)
        return (dq_out, dk_acc, dv_acc, score_store)

    start_carry = (
        jnp.zeros((seq_len, head_dim), jnp.float32),
        jnp.zeros((seq_len, head_dim), jnp.float32),
        jnp.zeros((seq_len, head_dim), jnp.float32),
        jnp.zeros((key_blocks, q_block, k_block), jnp.float32),
    )
    dq_out, dk_acc, dv_acc, score_store = lax.fori_loop(
        0, seq_len // q_block, query_step, start_carry
    )
    return (dq_out, dk_acc * score_scale, dv_acc)


def heads_plan(q_local, kv_local, d_local, segment_ids, segment_begin, vis_begin):
    tok_rows = q_local.shape[0]
    ctx_size = lax.axis_size("ctx")
    seq_len = tok_rows * ctx_size
    head_ratio = HEADS // KV_HEADS
    heads_here = HEADS // ctx_size
    d_part = d_local.reshape(1, tok_rows, HEADS, HEAD_DIM)
    packed = jnp.concatenate([head_layout(q_local, kv_local, head_ratio), d_part], axis=0)
    spread = lax.all_to_all(packed, "ctx", split_axis=2, concat_axis=1, tiled=True)

    def head_step(head_index, gradients):
        picked = lax.dynamic_index_in_dim(spread, head_index, 2, keepdims=False)
        head_dq, head_dk, head_dv = attend(
            picked[0], picked[1], picked[2], picked[3], segment_ids, segment_begin
        )
        update = jnp.stack([head_dq, head_dk, head_dv])[:, :, None, :]
        return update

    gradients = lax.fori_loop(
        0, heads_here, head_step, jnp.zeros((3, seq_len, heads_here, HEAD_DIM), jnp.float32)
    )
    image_part = lax.dynamic_slice_in_dim(gradients, vis_begin, VIS, 1)
    gradients = lax.dynamic_update_slice_in_dim(
        gradients, jnp.zeros((3, VIS, heads_here, HEAD_DIM), jnp.float32), vis_begin, 1
    )
    returned, returned_image = (
        lax.all_to_all(gradients, "ctx", split_axis=1, concat_axis=2, tiled=True),
        lax.all_to_all(image_part, "ctx", split_axis=1, concat_axis=2, tiled=True),
    )
    grad_q, grad_kv = fold_heads(returned, head_ratio)
    image_q, image_kv = fold_heads(returned_image, head_ratio)
    return (grad_q, grad_kv, jnp.concatenate([image_q, image_kv[0], image_kv[1]], axis=1))


def per_device(queries, keys_values, image_rows, cotangent, seq_image, vis_start, comp_lengths):
    tok_rows = queries.shape[1]
    ctx_size = lax.axis_size("ctx")
    ctx_place = lax.axis_index("ctx")
    group_place = lax.axis_index("rollout")
    seq_len = tok_rows * ctx_size
    query_width = HEADS * HEAD_DIM
    kv_width = KV_HEADS * HEAD_DIM
    prefix_len = VIS + PROMPT
    vis_begin = vis_start[0]
    owner_rows = lax.all_gather(image_rows, "rollout", axis=0, tiled=True)
    chosen = lax.dynamic_index_in_dim(owner_rows, seq_image[group_place], 0, keepdims=False)
    every_row = lax.all_gather(chosen, "ctx", axis=0, tiled=True)
    offset = ctx_place * tok_rows + jnp.arange(tok_rows, dtype=jnp.int32) - vis_begin
    inside = (offset >= 0) & (offset < VIS)
    picked_rows = jnp.take(every_row, jnp.clip(offset, 0, VIS - 1), axis=0)
    q_local = jnp.where(inside[:, None], picked_rows[:, :query_width], queries[0])
    fresh_kv = jnp.stack(
        [
            picked_rows[:, query_width : query_width + kv_width],
            picked_rows[:, query_width + kv_width :],
        ]
    )
    kv_local = jnp.where(inside[None, :, None], fresh_kv, keys_values[0])
    d_local = cotangent[0]
    seg_ends = jnp.cumsum(comp_lengths[0])
    positions = jnp.arange(seq_len, dtype=jnp.int32)
    later_ends = jnp.sum(
        (seg_ends[None, :] <= (positions - prefix_len)[:, None]).astype(jnp.int32), axis=1
    )
    segment_ids = jnp.where(positions < prefix_len, 0, 1 + later_ends)
    segment_begin = prefix_len + jnp.concatenate([jnp.zeros((1,), jnp.int32), seg_ends[:-1]])
    grad_q, grad_kv, image_grad = heads_plan(
        q_local, kv_local, d_local, segment_ids, segment_begin, vis_begin
    )
    group_grads = lax.all_gather(image_grad[None], "rollout", axis=0, tiled=True)
    user_group = jnp.sum(
        jnp.where(seq_image == group_place, jnp.arange(seq_image.shape[0], dtype=jnp.int32), 0)
    )
    own_grad = lax.dynamic_index_in_dim(group_grads, user_group, 0, keepdims=True)
    return (grad_q[None], grad_kv[None], own_grad)


def solution(mesh):
    placed = (
        P("rollout", "ctx", None),
        P("rollout", None, "ctx", None),
        P("rollout", "ctx", None),
        P("rollout", "ctx", None),
        P(),
        P("rollout"),
        P("rollout", None),
    )
    return jax.shard_map(
        per_device,
        mesh=mesh,
        in_specs=placed,
        out_specs=(
            P("rollout", "ctx", None),
            P("rollout", None, "ctx", None),
            P("rollout", "ctx", None),
        ),
        check_vma=False,
    )
```

profile of v0, /device:TPU:1, one launch (start us, length us, event | category | flops | bytes accessed | tf_op | source)
XLA Modules:
  0.0 1068.1 jit_solution(1359998070564322606)
XLA Ops:
  11.1 66.9 %all-gather.6.cloned.1.call-done = bf16[16,8,6144]{2,1,0:T(8,128)(2,1)} async-done(((bf16[1,8,6144]{2,1,0:T(8,128)(2,1)}), bf16[16,8,6144]{2,1,0:T(8,128)(2,1)}) %all-gather.6.cloned.1.call-update) | async-done | bytes 1572880 | tf_op jit(solution)/shard_map/all_gather | solution.py:193
  82.8 66.5 %all-gather.8.cloned.1.call-done = bf16[1,256,6144]{2,1,0:T(8,128)(2,1)} async-done(((bf16[1,8,6144]{2,1,0:T(8,128)(2,1)}), bf16[1,256,6144]{2,1,0:T(8,128)(2,1)}) %all-gather.8.cloned.1.call-update) | async-done | bytes 3145744 | tf_op jit(solution)/shard_map/all_gather | solution.py:195
  149.3 6.5 gather_fusion
  160.1 2.2 pad_maximum_fusion.1
  162.3 5.5 all-to-all-start
  169.5 48.5 %all-to-all-done = bf16[4,128,32,128]{3,1,0,2:T(8,128)(2,1)} async-done(((bf16[4,128,32,128]{3,1,0,2:T(8,128)(2,1)}), bf16[4,128,32,128]{3,1,0,2:T(8,128)(2,1)}, u32[]{:S(2)}, u32[]{:S(2)}) %all-to-all-start) | async-done | bytes 4194336 | tf_op jit(solution)/shard_map/all_to_all | solution.py:157
  218.1 4.0 fusion.57
  222.1 4.3 broadcast.219
  229.5 708.9 %while.323 = (s32[]{:T(128)}, f32[4096,128]{1,0:T(8,128)}, f32[4096,128]{1,0:T(8,128)S(1)}, f32[4096,128]{1,0:T(8,128)}, f32[32,512,128]{1,2,0:T(8,128)}, /*inde...) while((s32[]{:T(128)}, f32[4096,128]{1,0:T(8,128)}, ...), condition=%wide.region_17.18_spmd.clone.clone, body=%wide.region_2.17_spmd.clone.clone.sunk | while | flops 205525536 | bytes 9075373 | solution.py:143
  233.0 19.1 %while.324 = (s32[]{:T(128)}, f32[512]{0:T(512)S(1)}, f32[512]{0:T(512)S(1)}, f32[512]{0:T(512)S(1)}, f32[32,512,128]{1,2,0:T(8,128)}, /*index=5*/s32[]{:T(128)}...) while((s32[]{:T(128)}, f32[512]{0:T(512)S(1)}, ...), condition=%wide.region_7.7_spmd, body=%wide.region_3.6_spmd.sunk | while | flops 34998020 | bytes 1698917 | solution.py:102
  256.0 6.4 while.325
  262.4 10.6 while.326
  263.9 1.8 fusion.128
  273.0 3.5 while.327
  280.8 19.1 %while.324 = (s32[]{:T(128)}, f32[512]{0:T(512)S(1)}, f32[512]{0:T(512)S(1)}, f32[512]{0:T(512)S(1)}, f32[32,512,128]{1,2,0:T(8,128)}, /*index=5*/s32[]{:T(128)}...) while((s32[]{:T(128)}, f32[512]{0:T(512)S(1)}, ...), condition=%wide.region_7.7_spmd, body=%wide.region_3.6_spmd.sunk | while | flops 34998020 | bytes 1698917 | solution.py:102
  303.8 31.9 %while.325 = (s32[]{:T(128)}, f32[512]{0:T(512)S(1)}, f32[512]{0:T(512)S(1)}, f32[512]{0:T(512)S(1)}, f32[32,512,128]{1,2,0:T(8,128)}, /*index=5*/s32[]{:T(128)}...) while((s32[]{:T(128)}, f32[512]{0:T(512)S(1)}, ...), condition=%wide.region_12.12_spmd, body=%wide.region_8.11_spmd.sunk | while | flops 34998020 | bytes 1698917 | solution.py:103
  335.7 10.6 while.326
  337.1 1.8 fusion.128
  346.3 17.6 %while.327 = (s32[]{:T(128)}, f32[512,128]{1,0:T(8,128)S(1)}, f32[4096,128]{1,0:T(8,128)S(1)}, f32[4096,128]{1,0:T(8,128)}, s32[]{:T(128)}, /*index=5*/f32[32,51...) while((s32[]{:T(128)}, f32[512,128]{1,0:T(8,128)S(1)}, ...), condition=%wide.region_16.16_spmd, body=%wide.region_15.15_spmd.sunk | while | flops 67731464 | bytes 2173197 | solution.py:133
  354.8 1.8 fusion.139
  368.2 19.1 %while.324 = (s32[]{:T(128)}, f32[512]{0:T(512)S(1)}, f32[512]{0:T(512)S(1)}, f32[512]{0:T(512)S(1)}, f32[32,512,128]{1,2,0:T(8,128)}, /*index=5*/s32[]{:T(128)}...) while((s32[]{:T(128)}, f32[512]{0:T(512)S(1)}, ...), condition=%wide.region_7.7_spmd, body=%wide.region_3.6_spmd.sunk | while | flops 34998020 | bytes 1698917 | solution.py:102
  391.1 44.6 %while.325 = (s32[]{:T(128)}, f32[512]{0:T(512)S(1)}, f32[512]{0:T(512)S(1)}, f32[512]{0:T(512)S(1)}, f32[32,512,128]{1,2,0:T(8,128)}, /*index=5*/s32[]{:T(128)}...) while((s32[]{:T(128)}, f32[512]{0:T(512)S(1)}, ...), condition=%wide.region_12.12_spmd, body=%wide.region_8.11_spmd.sunk | while | flops 34998020 | bytes 1698917 | solution.py:103
  435.8 10.6 while.326
  446.4 24.7 %while.327 = (s32[]{:T(128)}, f32[512,128]{1,0:T(8,128)S(1)}, f32[4096,128]{1,0:T(8,128)S(1)}, f32[4096,128]{1,0:T(8,128)}, s32[]{:T(128)}, /*index=5*/f32[32,51...) while((s32[]{:T(128)}, f32[512,128]{1,0:T(8,128)S(1)}, ...), condition=%wide.region_16.16_spmd, body=%wide.region_15.15_spmd.sunk | while | flops 67731464 | bytes 2173197 | solution.py:133
  447.8 1.8 fusion.139
  458.4 1.8 fusion.139
  461.9 1.8 fusion.139
  475.4 19.1 %while.324 = (s32[]{:T(128)}, f32[512]{0:T(512)S(1)}, f32[512]{0:T(512)S(1)}, f32[512]{0:T(512)S(1)}, f32[32,512,128]{1,2,0:T(8,128)}, /*index=5*/s32[]{:T(128)}...) while((s32[]{:T(128)}, f32[512]{0:T(512)S(1)}, ...), condition=%wide.region_7.7_spmd, body=%wide.region_3.6_spmd.sunk | while | flops 34998020 | bytes 1698917 | solution.py:102
  498.3 38.2 %while.325 = (s32[]{:T(128)}, f32[512]{0:T(512)S(1)}, f32[512]{0:T(512)S(1)}, f32[512]{0:T(512)S(1)}, f32[32,512,128]{1,2,0:T(8,128)}, /*index=5*/s32[]{:T(128)}...) while((s32[]{:T(128)}, f32[512]{0:T(512)S(1)}, ...), condition=%wide.region_12.12_spmd, body=%wide.region_8.11_spmd.sunk | while | flops 34998020 | bytes 1698917 | solution.py:103
  536.6 10.6 while.326
  538.1 1.8 fusion.128
  547.2 21.1 %while.327 = (s32[]{:T(128)}, f32[512,128]{1,0:T(8,128)S(1)}, f32[4096,128]{1,0:T(8,128)S(1)}, f32[4096,128]{1,0:T(8,128)}, s32[]{:T(128)}, /*index=5*/f32[32,51...) while((s32[]{:T(128)}, f32[512,128]{1,0:T(8,128)S(1)}, ...), condition=%wide.region_16.16_spmd, body=%wide.region_15.15_spmd.sunk | while | flops 67731464 | bytes 2173197 | solution.py:133
  572.6 19.1 %while.324 = (s32[]{:T(128)}, f32[512]{0:T(512)S(1)}, f32[512]{0:T(512)S(1)}, f32[512]{0:T(512)S(1)}, f32[32,512,128]{1,2,0:T(8,128)}, /*index=5*/s32[]{:T(128)}...) while((s32[]{:T(128)}, f32[512]{0:T(512)S(1)}, ...), condition=%wide.region_7.7_spmd, body=%wide.region_3.6_spmd.sunk | while | flops 34998020 | bytes 1698917 | solution.py:102
  595.5 31.9 %while.325 = (s32[]{:T(128)}, f32[512]{0:T(512)S(1)}, f32[512]{0:T(512)S(1)}, f32[512]{0:T(512)S(1)}, f32[32,512,128]{1,2,0:T(8,128)}, /*index=5*/s32[]{:T(128)}...) while((s32[]{:T(128)}, f32[512]{0:T(512)S(1)}, ...), condition=%wide.region_12.12_spmd, body=%wide.region_8.11_spmd.sunk | while | flops 34998020 | bytes 1698917 | solution.py:103
  627.5 10.6 while.326
  629.0 1.8 fusion.128
  638.1 17.6 %while.327 = (s32[]{:T(128)}, f32[512,128]{1,0:T(8,128)S(1)}, f32[4096,128]{1,0:T(8,128)S(1)}, f32[4096,128]{1,0:T(8,128)}, s32[]{:T(128)}, /*index=5*/f32[32,51...) while((s32[]{:T(128)}, f32[512,128]{1,0:T(8,128)S(1)}, ...), condition=%wide.region_16.16_spmd, body=%wide.region_15.15_spmd.sunk | while | flops 67731464 | bytes 2173197 | solution.py:133
  660.0 19.1 %while.324 = (s32[]{:T(128)}, f32[512]{0:T(512)S(1)}, f32[512]{0:T(512)S(1)}, f32[512]{0:T(512)S(1)}, f32[32,512,128]{1,2,0:T(8,128)}, /*index=5*/s32[]{:T(128)}...) while((s32[]{:T(128)}, f32[512]{0:T(512)S(1)}, ...), condition=%wide.region_7.7_spmd, body=%wide.region_3.6_spmd.sunk | while | flops 34998020 | bytes 1698917 | solution.py:102
  682.9 44.7 %while.325 = (s32[]{:T(128)}, f32[512]{0:T(512)S(1)}, f32[512]{0:T(512)S(1)}, f32[512]{0:T(512)S(1)}, f32[32,512,128]{1,2,0:T(8,128)}, /*index=5*/s32[]{:T(128)}...) while((s32[]{:T(128)}, f32[512]{0:T(512)S(1)}, ...), condition=%wide.region_12.12_spmd, body=%wide.region_8.11_spmd.sunk | while | flops 34998020 | bytes 1698917 | solution.py:103
  727.6 10.6 while.326
  738.2 24.6 %while.327 = (s32[]{:T(128)}, f32[512,128]{1,0:T(8,128)S(1)}, f32[4096,128]{1,0:T(8,128)S(1)}, f32[4096,128]{1,0:T(8,128)}, s32[]{:T(128)}, /*index=5*/f32[32,51...) while((s32[]{:T(128)}, f32[512,128]{1,0:T(8,128)S(1)}, ...), condition=%wide.region_16.16_spmd, body=%wide.region_15.15_spmd.sunk | while | flops 67731464 | bytes 2173197 | solution.py:133
  760.8 1.8 fusion.139
  767.2 19.1 %while.324 = (s32[]{:T(128)}, f32[512]{0:T(512)S(1)}, f32[512]{0:T(512)S(1)}, f32[512]{0:T(512)S(1)}, f32[32,512,128]{1,2,0:T(8,128)}, /*index=5*/s32[]{:T(128)}...) while((s32[]{:T(128)}, f32[512]{0:T(512)S(1)}, ...), condition=%wide.region_7.7_spmd, body=%wide.region_3.6_spmd.sunk | while | flops 34998020 | bytes 1698917 | solution.py:102
  790.1 31.9 %while.325 = (s32[]{:T(128)}, f32[512]{0:T(512)S(1)}, f32[512]{0:T(512)S(1)}, f32[512]{0:T(512)S(1)}, f32[32,512,128]{1,2,0:T(8,128)}, /*index=5*/s32[]{:T(128)}...) while((s32[]{:T(128)}, f32[512]{0:T(512)S(1)}, ...), condition=%wide.region_12.12_spmd, body=%wide.region_8.11_spmd.sunk | while | flops 34998020 | bytes 1698917 | solution.py:103
  822.0 10.6 while.326
  832.6 17.6 %while.327 = (s32[]{:T(128)}, f32[512,128]{1,0:T(8,128)S(1)}, f32[4096,128]{1,0:T(8,128)S(1)}, f32[4096,128]{1,0:T(8,128)}, s32[]{:T(128)}, /*index=5*/f32[32,51...) while((s32[]{:T(128)}, f32[512,128]{1,0:T(8,128)S(1)}, ...), condition=%wide.region_16.16_spmd, body=%wide.region_15.15_spmd.sunk | while | flops 67731464 | bytes 2173197 | solution.py:133
  834.1 1.8 fusion.139
  841.1 1.8 fusion.139
  848.2 1.8 fusion.139
  854.5 19.1 %while.324 = (s32[]{:T(128)}, f32[512]{0:T(512)S(1)}, f32[512]{0:T(512)S(1)}, f32[512]{0:T(512)S(1)}, f32[32,512,128]{1,2,0:T(8,128)}, /*index=5*/s32[]{:T(128)}...) while((s32[]{:T(128)}, f32[512]{0:T(512)S(1)}, ...), condition=%wide.region_7.7_spmd, body=%wide.region_3.6_spmd.sunk | while | flops 34998020 | bytes 1698917 | solution.py:102
  877.5 31.9 %while.325 = (s32[]{:T(128)}, f32[512]{0:T(512)S(1)}, f32[512]{0:T(512)S(1)}, f32[512]{0:T(512)S(1)}, f32[32,512,128]{1,2,0:T(8,128)}, /*index=5*/s32[]{:T(128)}...) while((s32[]{:T(128)}, f32[512]{0:T(512)S(1)}, ...), condition=%wide.region_12.12_spmd, body=%wide.region_8.11_spmd.sunk | while | flops 34998020 | bytes 1698917 | solution.py:103
  909.5 10.6 while.326
  920.0 17.6 %while.327 = (s32[]{:T(128)}, f32[512,128]{1,0:T(8,128)S(1)}, f32[4096,128]{1,0:T(8,128)S(1)}, f32[4096,128]{1,0:T(8,128)}, s32[]{:T(128)}, /*index=5*/f32[32,51...) while((s32[]{:T(128)}, f32[512,128]{1,0:T(8,128)S(1)}, ...), condition=%wide.region_16.16_spmd, body=%wide.region_15.15_spmd.sunk | while | flops 67731464 | bytes 2173197 | solution.py:133
  921.5 1.8 fusion.139
  928.5 1.9 fusion.139
  940.6 3.5 pad_maximum_fusion
  945.3 7.2 all-to-all-start.2
  952.5 3.4 dynamic_update_slice.37
  955.9 8.6 copy.71
  964.5 7.5 all-to-all-start.1
  975.5 73.0 %all-gather.10.cloned.1.call-done = bf16[128,6144]{1,0:T(8,128)(2,1)} async-done(((bf16[8,6144]{1,0:T(8,128)(2,1)}), bf16[128,6144]{1,0:T(8,128)(2,1)}) %all-gather.10.cloned.1.call-update) | async-done | bytes 1572880 | tf_op jit(solution)/shard_map/all_gather | solution.py:218
  1050.1 3.2 copy.72
  1053.3 2.2 slice.103
  1055.7 2.6 reduce_sum.73
  (1386 shorter events, 685.3 us)
Async XLA Ops:
  7.2 74.2 %copy-start.6 = (bf16[1,128,4096]{2,1,0:T(8,128)(2,1)S(1)}, bf16[1,128,4096]{2,1,0:T(8,128)(2,1)}, u32[]{:S(2)}) copy-start(bf16[1,128,4096]{2,1,0:T(8,128)(2,1)} %param.20) | copy-start | bytes 3145732
  7.2 70.9 %all-gather.6.cloned.1.call-start = ((), (), s32[]{:S(2)}) async-start(), calls=%async_computation.3 | async-start | bytes 1671168 | tf_op jit(solution)/shard_map/all_gather | solution.py:193
  7.9 141.4 %all-gather.8.cloned.1.call-start = ((), (), s32[]{:S(2)}) async-start(), calls=%async_computation.4 | async-start | bytes 3244032 | tf_op jit(solution)/shard_map/all_gather | solution.py:195
  162.3 5.5 copy-start.10
  162.3 55.7 %all-to-all-start = ((bf16[4,128,32,128]{3,1,0,2:T(8,128)(2,1)}), bf16[4,128,32,128]{3,1,0,2:T(8,128)(2,1)}, u32[]{:S(2)}, u32[]{:S(2)}) async-start(bf16[4,128,32,128]{3,1,0,2:T(8,128)(2,1)} %pad_maximum_fusion.1), calls=%async_computation | async-start | bytes 8388608 | tf_op jit(solution)/shard_map/all_to_all | solution.py:157
  233.8 2.2 copy-start.3
  246.5 2.2 copy-start.3
  256.8 2.2 copy-start.5
  281.6 2.2 copy-start.3
  288.0 2.2 copy-start.3
  294.3 2.2 copy-start.3
  304.6 2.2 copy-start.5
  310.9 2.2 copy-start.5
  317.3 2.2 copy-start.5
  323.7 2.2 copy-start.5
  330.1 2.2 copy-start.5
  369.0 2.2 copy-start.3
  375.3 2.2 copy-start.3
  381.7 2.2 copy-start.3
  391.9 2.2 copy-start.5
  398.3 2.2 copy-start.5
  404.7 2.2 copy-start.5
  411.0 2.2 copy-start.5
  417.4 2.2 copy-start.5
  423.8 2.2 copy-start.5
  430.2 2.2 copy-start.5
  476.1 2.2 copy-start.3
  482.5 2.2 copy-start.3
  488.9 2.2 copy-start.3
  499.1 2.2 copy-start.5
  505.5 2.2 copy-start.5
  511.9 2.2 copy-start.5
  518.2 2.2 copy-start.5
  586.1 2.2 copy-start.3
  596.3 2.2 copy-start.5
  602.7 2.2 copy-start.5
  609.1 2.2 copy-start.5
  615.5 2.2 copy-start.5
  621.9 2.2 copy-start.5
  667.1 2.2 copy-start.3
  673.5 2.2 copy-start.3
  683.7 2.2 copy-start.5
  690.1 2.2 copy-start.5
  696.5 2.2 copy-start.5
  702.9 2.2 copy-start.5
  709.3 2.2 copy-start.5
  780.7 2.2 copy-start.3
  790.9 2.2 copy-start.5
  797.3 2.2 copy-start.5
  803.6 2.2 copy-start.5
  810.0 2.2 copy-start.5
  816.4 2.2 copy-start.5
  855.3 2.2 copy-start.3
  861.7 2.2 copy-start.3
  868.0 2.2 copy-start.3
  878.3 2.2 copy-start.5
  884.6 2.2 copy-start.5
  891.0 2.2 copy-start.5
  897.4 2.2 copy-start.5
  903.8 2.2 copy-start.5
  938.4 2.2 copy-start.1
  945.3 19.3 %all-to-all-start.2 = ((f32[3,256,1,128]{3,2,0,1:T(1,128)}), f32[3,256,1,128]{3,2,0,1:T(1,128)S(1)}, u32[]{:S(2)}, u32[]{:S(2)}) async-start(f32[3,256,1,128]{3,2,0,1:T(1,128)} %copy.76), calls=%async_computation.2 | async-start | bytes 786432 | tf_op jit(solution)/shard_map/all_to_all | solution.py:176
  964.5 85.6 %all-to-all-start.1 = ((f32[3,4096,1,128]{3,2,0,1:T(1,128)}), f32[3,4096,1,128]{3,2,0,1:T(1,128)}, u32[]{:S(2)}, u32[]{:S(2)}) async-start(f32[3,4096,1,128]{3,2,0,1:T(1,128)} %copy.71), calls=%async_computation.1 | async-start | bytes 12582912 | tf_op jit(solution)/shard_map/all_to_all | solution.py:175
  972.1 76.5 %all-gather.10.cloned.1.call-start = ((), (), s32[]{:S(2)}) async-start(), calls=%async_computation.5 | async-start | bytes 1671168 | tf_op jit(solution)/shard_map/all_gather | solution.py:218
  (143 other events, 166.5 us)
Sparse Core Ops, SparseCore 0:
  10.1 67.9 all-gather.5
  81.7 67.5 all-gather.7
  975.6 72.9 all-gather.9
where the time goes:
time: 1090 us; the launch traced here: 1070 us
  matrix products  395 us (36%)
  waiting for transfers between devices  256 us (23%)
  other arithmetic  218 us (20%)
  local copies, waits for them, and re-layouts  138 us (13%)
  loops' own time  22.8 us (2%)
  starting transfers between devices  20.3 us (2%)
  between operations  18.6 us (2%)
    dot_general x195, matrix products, contract_last(): lax.dot_general(left, right, (((1,), (1,)), ((), ())), preferred_element_...  250 us
    dot_general x130, matrix products, contract_first(): lax.dot_general(left, right, (((0,), (0,)), ((), ())), preferred_element_...  131 us
    all_gather x1, waiting for transfers between devices, per_device(): lax.all_gather(image_grad[None], 'rollout', axis=0, tiled=True)  73 us
    all_gather x1, waiting for transfers between devices, per_device(): owner_rows = lax.all_gather(image_rows, 'rollout', axis=0, tiled=True)  66.9 us
    all_gather x1, waiting for transfers between devices, per_device(): every_row = lax.all_gather(chosen, 'ctx', axis=0, tiled=True)  66.5 us
    reduce_sum x65, other arithmetic, stats_step(): jnp.sum(exp_terms, axis=1)  54.9 us
    eq x65, other arithmetic, stats_step(): seg_cols[None, :] == 0  49.9 us
    all_to_all x1, waiting for transfers between devices, heads_plan(): lax.all_to_all(packed, 'ctx', split_axis=2, concat_axis=1, tiled=True)  48.5 us
  transfers between devices with their start and end apart: 6, of which 4 were waited for; matrix products, arithmetic and copies ran while one was open for 2% of the time, Pallas kernels for 0%

commit v1 on v0

v1 whole, which is shorter than its diff:
```python
import functools
import math

import jax
import jax.numpy as jnp
from jax import lax
from jax.experimental import pallas as pl
from jax.experimental.pallas import tpu as pltpu
from jax.sharding import PartitionSpec as P

HEADS = 32
KV_HEADS = 8
HEAD_DIM = 128
VIS = 256
PROMPT = 64
PREFIX = VIS + PROMPT
GROUPS = 16
SHARDS = 32
CHIPS = 16
ROWS = 128
CHIP_ROWS = 256
HALO = 320
LOCAL = HALO + CHIP_ROWS
KEYS = PREFIX + LOCAL
QW = HEADS * HEAD_DIM // 2
KW = KV_HEADS * HEAD_DIM // 2
MESH = pl.DeviceIdType.MESH
BF = jnp.bfloat16
F32 = jnp.float32
NEG = -1e30


def remote(src, dst, send, recv, z, c):
    return pltpu.make_async_remote_copy(
        src_ref=src, dst_ref=dst, send_sem=send, recv_sem=recv, device_id=(z, c), device_id_type=MESH
    )


def arrived(ref, sem):
    pltpu.make_async_copy(ref, ref, sem).wait()


def each(count, body):
    def step(k, carry):
        body(k)
        return carry

    lax.fori_loop(0, count, step, 0)


def send_all(count, me, copy, local):
    def body(k):
        @pl.when(k != me)
        def _():
            copy(k).start()

        @pl.when(k == me)
        def _():
            local(k).start()

    each(count, body)


def sent_all(count, me, copy):
    def body(k):
        @pl.when(k != me)
        def _():
            copy(k).wait_send()

    each(count, body)


def greet(z, c):
    barrier = pltpu.get_barrier_semaphore()
    i = c // 2

    def plane(k):
        @pl.when(k != c)
        def _():
            pl.semaphore_signal(barrier, inc=1, device_id=(z, k), device_id_type=MESH)

    def column(k):
        @pl.when(k != z)
        def _():
            pl.semaphore_signal(barrier, inc=1, device_id=(k, 2 * i), device_id_type=MESH)
            pl.semaphore_signal(barrier, inc=1, device_id=(k, 2 * i + 1), device_id_type=MESH)

    each(SHARDS, plane)
    each(GROUPS, column)
    pl.semaphore_wait(barrier, SHARDS - 1 + 2 * (GROUPS - 1))


def gather_kernel(
    seq_ref, vis_ref, q, d, kv, img,
    q2, d2, kvloc, kvimg, kvtxt, imgq, imgd,
    z1buf, stage, z2buf, kvp, qp, ta, tb, tm, dv, ds,
    z1s, z2s, txs, sws, has, ags, ats, dss,
    z1r, z2r, tar, tbr, q2r, d2r, klr, kir, ktr, d0r, d1r, lcr,
):
    z = lax.axis_index("rollout")
    c = lax.axis_index("ctx")
    i = c // 2
    h = c % 2
    sib = 2 * i + 1 - h
    greet(z, c)

    def z1(j):
        return remote(img.at[j], z1buf.at[z], z1s.at[j], z1r, j, c)

    send_all(GROUPS, z, z1, lambda j: pltpu.make_async_copy(img.at[j], z1buf.at[z], z1r))

    def text_src(k):
        ii, hh = k // 2, k % 2
        b = ii % 8
        return kv.at[
            b // 4,
            pl.ds(pl.multiple_of(32 * (ii // 8), 32), 32),
            pl.ds(pl.multiple_of(KW * hh + 128 * (b % 4), 128), 128),
        ]

    for place, buf, sem in ((0, ta, tar), (2, tb, tbr)):
        @pl.when(c == place)
        def _():
            send_all(
                SHARDS, c,
                lambda k: remote(text_src(k), buf, txs.at[k], sem, z, k),
                lambda k: pltpu.make_async_copy(text_src(k), buf, sem),
            )

    def cols(core, width):
        return pl.ds(pl.multiple_of(width * core, width), width)

    my_rows = pl.ds(pl.multiple_of(ROWS * h, ROWS), ROWS)
    own_rows = pl.ds(pl.multiple_of(HALO + ROWS * h, 64), ROWS)
    near_rows = pl.ds(pl.multiple_of(64 + ROWS * h, 64), ROWS)
    swaps = [
        remote(d.at[:, cols(1 - h, QW)], d2.at[my_rows, :], sws.at[0], d2r, z, sib),
        remote(q.at[:, cols(1 - h, QW)], q2.at[my_rows, :], sws.at[1], q2r, z, sib),
        remote(kv.at[:, :, cols(1 - h, KW)], kvloc.at[:, own_rows, :], sws.at[2], klr, z, sib),
    ]
    one = lax.rem(i + 1, CHIPS)
    two = lax.rem(i + 2, CHIPS)
    swaps += [
        remote(kv.at[:, :, pl.ds(KW * hh, KW)], kvloc.at[:, near_rows, :], has.at[hh], klr, z, 2 * one + hh)
        for hh in (0, 1)
    ]
    far = [
        remote(
            kv.at[:, pl.ds(64, 64), pl.ds(KW * hh, KW)], kvloc.at[:, pl.ds(0, 64), :], has.at[2 + hh], klr, z,
            2 * two + hh,
        )
        for hh in (0, 1)
    ]
    for copy in swaps:
        copy.start()

    @pl.when(h == 1)
    def _():
        for copy in far:
            copy.start()

    pltpu.make_async_copy(d.at[:, cols(h, QW)], d2.at[my_rows, :], d2r).start()
    pltpu.make_async_copy(q.at[:, cols(h, QW)], q2.at[my_rows, :], q2r).start()
    pltpu.make_async_copy(kv.at[:, :, cols(h, KW)], kvloc.at[:, own_rows, :], klr).start()

    arrived(z1buf, z1r)

    def pick(g):
        stage[g] = z1buf[seq_ref[g]]

    each(GROUPS, pick)
    to_core = z % 2
    slot = 8 * h + z // 2
    here = jnp.where(to_core == h, z, GROUPS)

    def z2(g):
        return remote(stage.at[g], z2buf.at[slot], z2s.at[g], z2r, g, 2 * i + to_core)

    send_all(GROUPS, here, z2, lambda g: pltpu.make_async_copy(stage.at[g], z2buf.at[slot], z2r))

    arrived(ta, tar)
    arrived(tb, tbr)
    b = i % 8
    half = pl.ds(pl.multiple_of(32 * (i // 8), 32), 32)
    t = 32 * (i // 8) + lax.broadcasted_iota(jnp.int32, (32, 128), 0)
    tm[...] = jnp.where(t < vis_ref[0], ta[...].astype(F32), tb[...].astype(F32)).astype(BF)

    def atx(k):
        return remote(tm, kvtxt.at[b, half, :], ats.at[k], ktr, z, 2 * k + h)

    send_all(CHIPS, i, atx, lambda k: pltpu.make_async_copy(tm, kvtxt.at[b, half, :], ktr))

    def dsend(k):
        return remote(ds.at[pl.ds(pl.multiple_of(16 * k, 16), 16), :], imgd.at[0], dss.at[k], d0r, z, 2 * k + h)

    def dsend1(k):
        return remote(
            ds.at[pl.ds(pl.multiple_of(192 + 16 * k, 16), 16), :], imgd.at[1], dss.at[k], d1r, z, 2 * (12 + k) + h
        )

    @pl.when(i < 2)
    def _():
        arrived(d2, d2r)
        load = pltpu.make_async_copy(d2, dv, lcr)
        load.start()
        load.wait()
        r = lax.broadcasted_iota(jnp.int32, (VIS, CHIP_ROWS), 0)
        p = lax.broadcasted_iota(jnp.int32, (VIS, CHIP_ROWS), 1)
        pick_rows = jnp.where(p + CHIP_ROWS * i == r + vis_ref[0], 1.0, 0.0).astype(BF)
        for part in range(4):
            w = pl.ds(part * 512, 512)
            ds[:, w] = jnp.dot(pick_rows, dv[:, w], preferred_element_type=F32).astype(BF)

    @pl.when(i == 0)
    def _():
        send_all(CHIPS, i, dsend, lambda k: pltpu.make_async_copy(ds.at[pl.ds(0, 16), :], imgd.at[0], d0r))

    @pl.when(i == 1)
    def _():
        each(4, lambda k: dsend1(k).start())

    arrived(z2buf, z2r)
    o = lax.broadcasted_iota(jnp.int32, (384, 512), 0)
    n = lax.broadcasted_iota(jnp.int32, (384, 512), 1)
    perm = jnp.where(n == (o % 16) * 32 + o // 16, 1.0, 0.0).astype(BF)
    by_head = jnp.dot(perm, z2buf[...].reshape(512, 128), preferred_element_type=F32).astype(BF).reshape(24, 16, 128)
    qp[...] = by_head[:16]
    kvp[...] = by_head[16:]
    mine = pl.ds(pl.multiple_of(16 * i, 16), 16)

    def aim(k):
        return remote(kvp, kvimg.at[:, mine, :], ags.at[k], kir, z, 2 * k + h)

    send_all(CHIPS, i, aim, lambda k: pltpu.make_async_copy(kvp, kvimg.at[:, mine, :], kir))
    out_q = pltpu.make_async_copy(qp, imgq, lcr)
    out_q.start()

    arrived(q2, q2r)

    @pl.when(i >= 2)
    def _():
        arrived(d2, d2r)

    arrived(kvloc, klr)
    arrived(kvtxt, ktr)
    arrived(imgd.at[0], d0r)

    @pl.when(i >= 12)
    def _():
        arrived(imgd.at[1], d1r)

    arrived(kvimg, kir)
    out_q.wait()

    sent_all(GROUPS, z, z1)
    sent_all(GROUPS, here, z2)
    for place, buf, sem in ((0, ta, tar), (2, tb, tbr)):
        @pl.when(c == place)
        def _():
            sent_all(SHARDS, c, lambda k: remote(text_src(k), buf, txs.at[k], sem, z, k))

    for copy in swaps:
        copy.wait_send()

    @pl.when(h == 1)
    def _():
        for copy in far:
            copy.wait_send()

    sent_all(CHIPS, i, atx)
    sent_all(CHIPS, i, aim)

    @pl.when(i == 0)
    def _():
        sent_all(CHIPS, i, dsend)

    @pl.when(i == 1)
    def _():
        each(4, lambda k: dsend1(k).wait_send())


def attend_kernel(
    vis_ref, len_ref, q, d, kvloc, kvimg, kvtxt, imgq, imgd,
    dq, dkvloc, dkvimg, dkvtxt, dimgq,
    bias, ibias, valid, kall, vall, kt, dk, dv,
):
    i = lax.axis_index("ctx") // 2
    scale = 1.0 / math.sqrt(HEAD_DIM)
    to_log2 = scale * math.log2(math.e)
    vis = vis_ref[0]

    @pl.when(pl.program_id(0) == 0)
    def _():
        def slot_positions(lanes):
            r = lax.broadcasted_iota(jnp.int32, (PREFIX, lanes), 0)
            text = r - VIS
            return jnp.where(r < VIS, vis + r, jnp.where(text < vis, text, r))

        pos = CHIP_ROWS * i + lax.broadcasted_iota(jnp.int32, (1, CHIP_ROWS), 1)
        begin = jnp.full((1, CHIP_ROWS), PREFIX, jnp.int32)
        edge = jnp.int32(PREFIX)
        for k in range(16):
            edge = edge + len_ref[0, k]
            begin = jnp.where(pos >= edge, edge, begin)
        begin = jnp.where(pos < PREFIX, pos + 1, begin)
        valid[...] = jnp.where((pos >= vis) & (pos < vis + VIS), 0.0, 1.0)
        bias[:PREFIX, :] = jnp.where(slot_positions(CHIP_ROWS) <= pos, 0.0, NEG)
        at = CHIP_ROWS * i - HALO + lax.broadcasted_iota(jnp.int32, (LOCAL, CHIP_ROWS), 0)
        bias[PREFIX:, :] = jnp.where((at >= begin) & (at <= pos), 0.0, NEG)
        ipos = vis + 16 * i + lax.broadcasted_iota(jnp.int32, (1, 64), 1) % 16
        ibias[...] = jnp.where(slot_positions(64) <= ipos, 0.0, NEG)

    for whole, index in ((kall, 0), (vall, 1)):
        whole[:VIS, :] = kvimg[index, 0]
        whole[VIS:PREFIX, :] = kvtxt[index, 0]
        whole[PREFIX:, :] = kvloc[index]
    kt[...] = kall[...].T
    nt = (((1,), (1,)), ((), ()))

    def grads(k_rows, v_rows, q_rows, d_rows, mask, live):
        top = lax.dot_general(k_rows, q_rows, nt, preferred_element_type=F32) * to_log2 + mask
        e = jnp.exp2(top - jnp.max(top, axis=0, keepdims=True))
        dw = lax.dot_general(v_rows, d_rows, nt, preferred_element_type=F32)
        inv = 1.0 / jnp.sum(e, axis=0, keepdims=True)
        delta = jnp.sum(e * dw, axis=0, keepdims=True) * inv
        if live is not None:
            inv = inv * live
        w = e * inv
        s = (w * (dw - delta)).astype(BF)
        return s, w.astype(BF)

    qi = imgq[...].reshape(64, 128)
    di0 = imgd[0].astype(F32)
    di1 = jnp.where(i >= 12, imgd[1].astype(F32), 0.0)
    di = (di0 + di1).astype(BF)
    di = jnp.concatenate([di[:, 128 * k : 128 * (k + 1)] for k in range(4)], axis=0)
    s, w = grads(kall[:PREFIX, :], vall[:PREFIX, :], qi, di, ibias[...], None)
    dk[:PREFIX, :] = jnp.dot(s, qi, preferred_element_type=F32)
    dv[:PREFIX, :] = jnp.dot(w, di, preferred_element_type=F32)
    dk[PREFIX:, :] = jnp.zeros((LOCAL, 128), F32)
    dv[PREFIX:, :] = jnp.zeros((LOCAL, 128), F32)
    dqi = jnp.dot(kt[:, :PREFIX], s, preferred_element_type=F32) * scale
    dimgq[...] = dqi.T.astype(BF).reshape(4, 16, 128)

    for k in range(4):
        w128 = pl.ds(128 * k, 128)
        qh = q[:, w128]
        dh = d[:, w128]
        s, w = grads(kall[...], vall[...], qh, dh, bias[...], valid[...])
        dk[...] += jnp.dot(s, qh, preferred_element_type=F32)
        dv[...] += jnp.dot(w, dh, preferred_element_type=F32)
        dqt = jnp.dot(kt[...], s, preferred_element_type=F32) * scale
        dq[:, w128] = dqt.T.astype(BF)

    for index, part, factor in ((0, dk, scale), (1, dv, 1.0)):
        total = (part[...] * factor).astype(BF)
        dkvimg[index, 0] = total[:VIS]
        dkvtxt[index, 0] = total[VIS:PREFIX]
        dkvloc[index] = total[PREFIX:]


def scatter_kernel(
    inv_ref, vis_ref, dq2, dkvloc, dkvimg, dkvtxt, dimgq,
    gq, gkv, gimg,
    rsi, rst, hb0, hb1, hb2, dtx, heads, rows, zb, stage, tx, kvo,
    ris, rts, hs, qs, xs, z1s, z2s,
    rir, rtr, h0r, h1r, h2r, gqr, xr, z1r, z2r, lcr,
):
    z = lax.axis_index("rollout")
    c = lax.axis_index("ctx")
    i = c // 2
    h = c % 2
    sib = 2 * i + 1 - h
    greet(z, c)

    def block(k):
        return pl.ds(pl.multiple_of(16 * k, 16), 16)

    def half_of(k):
        return pl.ds(pl.multiple_of(32 * (k // 8), 32), 32)

    load = pltpu.make_async_copy(dimgq, heads.at[pl.ds(0, 16)], lcr)
    load.start()

    def rimg(k):
        return remote(dkvimg.at[:, block(k), :], rsi.at[i], ris.at[k], rir, z, 2 * k + h)

    def rtxt(k):
        return remote(dkvtxt.at[k % 8, half_of(k), :], rst.at[i], rts.at[k], rtr, z, 2 * k + h)

    send_all(CHIPS, i, rimg, lambda k: pltpu.make_async_copy(dkvimg.at[:, block(k), :], rsi.at[i], rir))
    send_all(CHIPS, i, rtxt, lambda k: pltpu.make_async_copy(dkvtxt.at[k % 8, half_of(k), :], rst.at[i], rtr))

    one = lax.rem(i + CHIPS - 1, CHIPS)
    two = lax.rem(i + CHIPS - 2, CHIPS)

    def rows_of(core, first):
        return pl.ds(pl.multiple_of(first + ROWS * core, 64), ROWS)

    my_cols = pl.ds(pl.multiple_of(QW * h, QW), QW)
    copies = [
        remote(dkvloc.at[:, rows_of(s, 64), :], hb1.at[h], hs.at[s], h1r, z, 2 * one + s) for s in (0, 1)
    ] + [
        remote(dkvloc.at[:, pl.ds(0, 64), :], hb2.at[h], hs.at[2], h2r, z, 2 * two + 1),
        remote(dkvloc.at[:, rows_of(1 - h, HALO), :], hb0.at[h], hs.at[3], h0r, z, sib),
        remote(dq2.at[rows_of(1 - h, 0), :], gq.at[:, my_cols], qs, gqr, z, sib),
    ]
    for copy in copies:
        copy.start()
    pltpu.make_async_copy(dkvloc.at[:, rows_of(h, HALO), :], hb0.at[h], h0r).start()
    pltpu.make_async_copy(dq2.at[rows_of(h, 0), :], gq.at[:, my_cols], gqr).start()

    arrived(rst, rtr)
    total = rst[0].astype(F32)
    for k in range(1, CHIPS):
        total = total + rst[k].astype(F32)
    tx[...] = total.astype(BF)
    txt_slot = dtx.at[h, i % 8, half_of(i), :]

    for n, place in ((0, 0), (1, 2)):
        @pl.when(c != place)
        def _():
            remote(tx, txt_slot, xs.at[n], xr, z, place).start()

        @pl.when(c == place)
        def _():
            pltpu.make_async_copy(tx, txt_slot, xr).start()

    arrived(rsi, rir)
    total = rsi[0].astype(F32)
    for k in range(1, CHIPS):
        total = total + rsi[k].astype(F32)
    load.wait()
    heads[16:] = total.astype(BF)

    o = lax.broadcasted_iota(jnp.int32, (512, 384), 0)
    n = lax.broadcasted_iota(jnp.int32, (512, 384), 1)
    perm = jnp.where(n == (o % 32) * 16 + o // 32, 1.0, 0.0).astype(BF)
    rows[...] = (
        jnp.dot(perm, heads[...].reshape(384, 128), preferred_element_type=F32).astype(BF).reshape(16, 32, 128)
    )
    here = jnp.where(z % 2 == h, 8 * h + z // 2, GROUPS)

    def z1(r):
        return remote(rows.at[r], zb.at[z], z1s.at[r], z1r, 2 * (r % 8) + h, 2 * i + r // 8)

    send_all(16, here, z1, lambda r: pltpu.make_async_copy(rows.at[r], zb.at[z], z1r))
    arrived(zb, z1r)

    def pick(g):
        stage[g] = zb[inv_ref[g]]

    each(GROUPS, pick)

    def z2(g):
        return remote(stage.at[g], gimg.at[z], z2s.at[g], z2r, g, c)

    send_all(GROUPS, z, z2, lambda g: pltpu.make_async_copy(stage.at[g], gimg.at[z], z2r))

    arrived(hb0, h0r)
    arrived(hb1, h1r)

    @pl.when(h == 1)
    def _():
        arrived(hb2, h2r)

    for hh in (0, 1):
        for n in (0, 1):
            w = pl.ds(KW * hh, KW)
            near = hb0[hh, n].astype(F32) + hb1[hh, n].astype(F32)
            kvo[n, :64, w] = near[:64].astype(BF)
            more = jnp.where(h == 1, hb2[hh, n].astype(F32), 0.0)
            kvo[n, 64:, w] = (near[64:] + more).astype(BF)

    t = lax.broadcasted_iota(jnp.int32, (PROMPT, 128), 0)
    vis = vis_ref[0]
    for place in (0, 2):
        @pl.when(c == place)
        def _():
            arrived(dtx, xr)
            keep = t < vis if place == 0 else t >= vis
            for hh in (0, 1):
                for b in range(8):
                    kvo[b // 4, :64, pl.ds(KW * hh + 128 * (b % 4), 128)] = jnp.where(
                        keep, dtx[hh, b].astype(F32), 0.0
                    ).astype(BF)

    out = pltpu.make_async_copy(kvo, gkv, lcr)
    out.start()
    arrived(gq, gqr)
    arrived(gimg, z2r)
    out.wait()

    sent_all(CHIPS, i, rimg)
    sent_all(CHIPS, i, rtxt)
    for copy in copies:
        copy.wait_send()
    for n, place in ((0, 0), (1, 2)):
        @pl.when(c != place)
        def _():
            remote(tx, txt_slot, xs.at[n], xr, z, place).wait_send()

    sent_all(16, here, z1)
    sent_all(GROUPS, z, z2)


ANY = pl.BlockSpec(memory_space=pl.ANY)
SMEM = pl.BlockSpec(memory_space=pltpu.SMEM)
DMA = pltpu.SemaphoreType.DMA


def sds(*shape):
    return jax.ShapeDtypeStruct(shape, BF)


def vm(*shape, dtype=BF):
    return pltpu.VMEM(shape, dtype)


def per_device(queries, keys_values, image_rows, cotangent, seq_image, vis_start, comp_lengths):
    rows = image_rows[0]
    q_part = rows[:, : 2 * QW].reshape(8, 2, 16, 128)
    k_part = rows[:, 2 * QW : 2 * QW + 2 * KW].reshape(8, 2, 4, 128)
    v_part = rows[:, 2 * QW + 2 * KW :].reshape(8, 2, 4, 128)
    pieces = jnp.concatenate([q_part, k_part, v_part, jnp.zeros((8, 2, 8, 128), BF)], axis=2)
    pieces = pieces.reshape(16, 32, 128)

    q2, d2, kvloc, kvimg, kvtxt, imgq, imgd = pl.pallas_call(
        gather_kernel,
        out_shape=[
            sds(CHIP_ROWS, QW), sds(CHIP_ROWS, QW), sds(2, LOCAL, KW), sds(8, VIS, 128), sds(8, PROMPT, 128),
            sds(16, 16, 128), sds(2, 16, QW),
        ],
        in_specs=[SMEM, SMEM, ANY, ANY, ANY, ANY],
        out_specs=[ANY] * 7,
        scratch_shapes=[
            vm(16, 32, 128), vm(16, 32, 128), vm(16, 32, 128), vm(8, 16, 128), vm(16, 16, 128),
            vm(32, 128), vm(32, 128), vm(32, 128), vm(CHIP_ROWS, QW), vm(CHIP_ROWS, QW),
            DMA((16,)), DMA((16,)), DMA((32,)), DMA((3,)), DMA((4,)), DMA((16,)), DMA((16,)), DMA((16,)),
        ] + [DMA(())] * 12,
        compiler_params=pltpu.CompilerParams(
            collective_id=0, has_side_effects=True, vmem_limit_bytes=32 * 2**20
        ),
        name="gather_in",
    )(seq_image, vis_start, queries[0], cotangent[0], keys_values[0], pieces)

    dq2, dkvloc, dkvimg, dkvtxt, dimgq = pl.pallas_call(
        attend_kernel,
        grid=(4,),
        out_shape=[
            sds(CHIP_ROWS, QW), sds(2, LOCAL, KW), sds(2, 4, VIS, 128), sds(2, 4, PROMPT, 128), sds(16, 16, 128),
        ],
        in_specs=[
            SMEM, SMEM,
            pl.BlockSpec((CHIP_ROWS, 512), lambda e: (0, e)),
            pl.BlockSpec((CHIP_ROWS, 512), lambda e: (0, e)),
            pl.BlockSpec((2, LOCAL, 128), lambda e: (0, 0, e)),
            pl.BlockSpec((2, 1, VIS, 128), lambda e: (0, e, 0, 0)),
            pl.BlockSpec((2, 1, PROMPT, 128), lambda e: (0, e, 0, 0)),
            pl.BlockSpec((4, 16, 128), lambda e: (e, 0, 0)),
            pl.BlockSpec((2, 16, 512), lambda e: (0, 0, e)),
        ],
        out_specs=[
            pl.BlockSpec((CHIP_ROWS, 512), lambda e: (0, e)),
            pl.BlockSpec((2, LOCAL, 128), lambda e: (0, 0, e)),
            pl.BlockSpec((2, 1, VIS, 128), lambda e: (0, e, 0, 0)),
            pl.BlockSpec((2, 1, PROMPT, 128), lambda e: (0, e, 0, 0)),
            pl.BlockSpec((4, 16, 128), lambda e: (e, 0, 0)),
        ],
        scratch_shapes=[
            vm(KEYS, CHIP_ROWS, dtype=F32), vm(PREFIX, 64, dtype=F32), vm(1, CHIP_ROWS, dtype=F32),
            vm(KEYS, 128), vm(KEYS, 128), vm(128, KEYS), vm(KEYS, 128, dtype=F32), vm(KEYS, 128, dtype=F32),
        ],
        compiler_params=pltpu.CompilerParams(vmem_limit_bytes=48 * 2**20),
        name="attend",
    )(
        vis_start, comp_lengths, q2, d2, kvloc, kvimg.reshape(2, 4, VIS, 128), kvtxt.reshape(2, 4, PROMPT, 128),
        imgq, imgd,
    )

    groups = jnp.arange(GROUPS, dtype=jnp.int32)
    user = jnp.sum(jnp.where(seq_image[None, :] == groups[:, None], groups[None, :], 0), axis=1, dtype=jnp.int32)
    gq, gkv, gimg = pl.pallas_call(
        scatter_kernel,
        out_shape=[sds(ROWS, 2 * QW), sds(2, ROWS, 2 * KW), sds(16, 32, 128)],
        in_specs=[SMEM, SMEM] + [ANY] * 5,
        out_specs=[ANY] * 3,
        scratch_shapes=[
            vm(16, 8, 16, 128), vm(16, 32, 128), vm(2, 2, ROWS, KW), vm(2, 2, ROWS, KW), vm(2, 2, 64, KW),
            vm(2, 8, 64, 128), vm(24, 16, 128), vm(16, 32, 128), vm(16, 32, 128), vm(16, 32, 128), vm(32, 128),
            vm(2, ROWS, 2 * KW),
            DMA((16,)), DMA((16,)), DMA((4,)), DMA(()), DMA((2,)), DMA((16,)), DMA((16,)),
        ] + [DMA(())] * 10,
        compiler_params=pltpu.CompilerParams(
            collective_id=1, has_side_effects=True, vmem_limit_bytes=32 * 2**20
        ),
        name="scatter_out",
    )(user, vis_start, dq2, dkvloc, dkvimg.reshape(8, VIS, 128), dkvtxt.reshape(8, PROMPT, 128), dimgq)

    gimg = gimg.reshape(8, 2, 32, 128)
    own = jnp.concatenate(
        [
            gimg[:, :, :16].reshape(8, 2 * QW),
            gimg[:, :, 16:20].reshape(8, 2 * KW),
            gimg[:, :, 20:24].reshape(8, 2 * KW),
        ],
        axis=1,
    )
    return (gq[None], gkv[None], own[None])


def solution(mesh):
    placed = (
        P("rollout", "ctx", None),
        P("rollout", None, "ctx", None),
        P("rollout", "ctx", None),
        P("rollout", "ctx", None),
        P(),
        P("rollout"),
        P("rollout", None),
    )
    return jax.shard_map(
        per_device,
        mesh=mesh,
        in_specs=placed,
        out_specs=(
            P("rollout", "ctx", None),
            P("rollout", None, "ctx", None),
            P("rollout", "ctx", None),
        ),
        check_vma=False,
    )
```

time: 1090 us -> 120 us (0.11); the launches traced: 1070 us -> 120 us
  matrix products: 395 us -> 0 us
  waiting for transfers between devices: 256 us -> 0 us
  other arithmetic: 218 us -> 0.86 us
  local copies, waits for them, and re-layouts: 138 us -> 8.74 us
  Pallas kernels: 0 us -> 109 us
  loops' own time: 22.8 us -> 0 us
  starting transfers between devices: 20.3 us -> 0 us
  between operations: 18.6 us -> 1.4 us
    dot_general x390 -> x0, matrix products: 395 us -> none  [the longest x195 250 us: contract_last(): lax.dot_general(left, right, (((1,), (1,)), ((), ())), preferred_element_...]
    all_gather x3 -> x0, waiting for transfers between devices: 206 us -> none  [the longest x1 73 us: per_device(): lax.all_gather(image_grad[None], 'rollout', axis=0, tiled=True)]
    pallas_call x0 -> x3, Pallas kernels: none -> 109 us  [the longest x1 52.2 us: per_device(): pl.pallas_call(gather_kernel, out_shape=[sds(CHIP_ROWS, QW), sds(CHIP_ROW...]
    dynamic_update_slice x67 -> x0, local copies, waits for them, and re-layouts: 58.6 us -> none  [the longest x65 46.6 us: stats_step(): stored = lax.dynamic_update_index_in_dim(stored, scores, key_index, 0)]
    reduce_sum x69 -> x1, other arithmetic: 58.3 us -> 0.11 us  [per_device(): jnp.sum(jnp.where(seq_image[None, :] == groups[:, None], groups[None, :],...]
    add x139 -> x0, other arithmetic: 49.9 us -> none  [the longest x65 43.5 us: stats_step(): k_begin + column_ids]
    eq x65 -> x0, other arithmetic: 49.9 us -> none  [stats_step(): seg_cols[None, :] == 0]
    all_to_all x3 -> x0, waiting for transfers between devices: 48.5 us -> none  [the longest x1 48.5 us: heads_plan(): lax.all_to_all(packed, 'ctx', split_axis=2, concat_axis=1, tiled=True)]
  transfers between devices with their start and end apart: 6 -> 0, of which waited for: 4 -> 0; matrix products, arithmetic and copies ran while one was open for 2% -> 0% of each run, Pallas kernels for 0% -> 0%
where the time goes in v1:
time: 120 us
  Pallas kernels  109 us (91%)
  local copies, waits for them, and re-layouts  8.74 us (7%)
  between operations  1.4 us (1%)
    pallas_call x1, Pallas kernels, per_device(): pl.pallas_call(gather_kernel, out_shape=[sds(CHIP_ROWS, QW), sds(CHIP_ROW...  52.2 us
    pallas_call x1, Pallas kernels, per_device(): pl.pallas_call(scatter_kernel, out_shape=[sds(ROWS, 2 * QW), sds(2, ROWS,...  37.2 us
    pallas_call x1, Pallas kernels, per_device(): pl.pallas_call(attend_kernel, grid=(4,), out_shape=[sds(CHIP_ROWS, QW), s...  19.1 us
    unnamed x17, local copies, waits for them, and re-layouts  6.96 us

profile of v1, /device:TPU:1, one launch (start us, length us, event | category | flops | bytes accessed | tf_op | source)
XLA Modules:
  0.0 119.6 jit_solution(11891478745387992539)
XLA Ops:
  0.6 0.7 fusion.1
  1.4 0.8 slice.24
  2.3 0.1 pad.6.clone
  2.4 0.1 maximum_maximum_fusion.img
  3.1 0.0 copy-start.1
  3.1 1.2 %copy-done.1 = bf16[1,128,4096]{2,1,0:T(8,128)(2,1)S(1)} copy-done((bf16[1,128,4096]{2,1,0:T(8,128)(2,1)S(1)}, bf16[1,128,4096]{2,1,0:T(8,128)(2,1)}, u32[]{:S(2)}) %copy-start.1) | copy-done | bytes 1048600
  4.4 0.0 copy-start.2
  4.4 1.2 %copy-done.2 = bf16[1,128,4096]{2,1,0:T(8,128)(2,1)S(1)} copy-done((bf16[1,128,4096]{2,1,0:T(8,128)(2,1)S(1)}, bf16[1,128,4096]{2,1,0:T(8,128)(2,1)}, u32[]{:S(2)}) %copy-start.2) | copy-done | bytes 1048600
  5.6 0.0 copy-start.3
  5.6 1.0 copy-done.3
  6.6 0.0 copy-start.5
  6.6 0.7 copy-done.5
  7.3 0.0 copy-start.4
  7.3 52.2 %gather_in.1 = (bf16[256,2048]{1,0:T(8,128)(2,1)S(1)}, bf16[256,2048]{1,0:T(8,128)(2,1)S(1)}, bf16[2,576,512]{2,1,0:T(8,128)(2,1)S(1)}, bf16[8,256,128]{2,1,0:T(...) custom-call(s32[16]{0:T(128)S(1)} %copy-done.5, ...), custom_call_target="tpu_custom_call" | custom-call | tf_op jit(solution)/shard_map/gather_in/pallas_call | solution.py:528
  59.5 0.0 copy-start
  59.5 1.0 copy-done
  60.6 0.0 copy-done.4
  60.6 0.0 copy-start.6
  60.6 19.1 %attend.1 = (bf16[256,2048]{1,0:T(8,128)(2,1)S(1)}, bf16[2,576,512]{2,1,0:T(8,128)(2,1)S(1)}, bf16[2,4,256,128]{3,2,1,0:T(8,128)(2,1)S(1)}, bf16[2,4,64,128]{3,2,1,0:T(8,128)(2,1)S(1)}, bf16[16,16,128]{2,1,0:T(8,128)(2,1)S(1)}) custom-call(s32[1]{0:T(128)S(6)} %copy.15.vis_ref, s32[1,16]{1,0:T(1,128)S(1)} %copy-done.4, ...), custom_call_target="tpu_custom_call" | custom-call | tf_op jit(solution)/shard_map/attend/pallas_call | solution.py:547
  79.7 0.0 copy-done.6
  79.7 0.1 select_reduce_fusion.inv_ref
  79.8 37.2 %scatter_out.1 = (bf16[128,4096]{1,0:T(8,128)(2,1)S(1)}, bf16[2,128,1024]{2,1,0:T(8,128)(2,1)S(1)}, bf16[16,32,128]{2,1,0:T(8,128)(2,1)S(1)}) custom-call(s32[16]{0:T(128)S(1)} %select_reduce_fusion.inv_ref, s32[1]{0:T(128)S(6)} %copy.15.vis_ref, bf16[256,2048]{1,0:T(8,128)(2,1)S(1)} %get-tuple-element.25.dq2, ...), custom_call_target="tpu_custom_call" | custom-call | tf_op jit(solution)/shard_map/scatter_out/pallas_call | solution.py:583
  117.1 0.6 maximum_bitcast_fusion
  117.8 1.0 copy.16
  118.8 0.8 copy.17
  (9 shorter events, 0.1 us)
Async XLA Ops:
  3.1 1.2 %copy-start.1 = (bf16[1,128,4096]{2,1,0:T(8,128)(2,1)S(1)}, bf16[1,128,4096]{2,1,0:T(8,128)(2,1)}, u32[]{:S(2)}) copy-start(bf16[1,128,4096]{2,1,0:T(8,128)(2,1)} %param.7) | copy-start | bytes 3145732
  4.4 1.2 %copy-start.2 = (bf16[1,128,4096]{2,1,0:T(8,128)(2,1)S(1)}, bf16[1,128,4096]{2,1,0:T(8,128)(2,1)}, u32[]{:S(2)}) copy-start(bf16[1,128,4096]{2,1,0:T(8,128)(2,1)} %param.10) | copy-start | bytes 3145732
  5.6 1.0 copy-start.3
  6.6 0.7 copy-start.5
  7.3 53.3 %copy-start.4 = (s32[1,16]{1,0:T(1,128)S(1)}, s32[1,16]{1,0:T(1,128)}, u32[]{:S(2)}) copy-start(s32[1,16]{1,0:T(1,128)} %len_ref.1) | copy-start | bytes 196
  59.5 1.0 copy-start
  60.6 19.1 %copy-start.6 = (s32[16]{0:T(128)S(1)}, s32[16]{0:T(128)}, u32[]{:S(2)}) copy-start(s32[16]{0:T(128)} %seq_ref.1) | copy-start | bytes 196

commit v2 on v1

v2 whole, which is shorter than its diff:
```python
import functools
import math

import jax
import jax.numpy as jnp
from jax import lax
from jax.experimental import pallas as pl
from jax.experimental.pallas import tpu as pltpu
from jax.sharding import PartitionSpec as P

HEADS = 32
KV_HEADS = 8
HEAD_DIM = 128
VIS = 256
PROMPT = 64
PREFIX = VIS + PROMPT
GROUPS = 16
SHARDS = 32
CHIPS = 16
ROWS = 128
CHIP_ROWS = 256
HALO = 320
LOCAL = HALO + CHIP_ROWS
KEYS = PREFIX + LOCAL
QW = HEADS * HEAD_DIM // 2
KW = KV_HEADS * HEAD_DIM // 2
MESH = pl.DeviceIdType.MESH
BF = jnp.bfloat16
F32 = jnp.float32
NEG = -1e30
RS_AT = 2


def remote(src, dst, send, recv, z, c):
    return pltpu.make_async_remote_copy(
        src_ref=src, dst_ref=dst, send_sem=send, recv_sem=recv, device_id=(z, c), device_id_type=MESH
    )


def arrived(ref, sem):
    pltpu.make_async_copy(ref, ref, sem).wait()


def each(count, body):
    def step(k, carry):
        body(k)
        return carry

    lax.fori_loop(0, count, step, 0)


def send_all(count, me, copy, local):
    def body(k):
        @pl.when(k != me)
        def _():
            copy(k).start()

        @pl.when(k == me)
        def _():
            local(k).start()

    each(count, body)


def sent_all(count, me, copy):
    def body(k):
        @pl.when(k != me)
        def _():
            copy(k).wait_send()

    each(count, body)


def greet(z, c):
    barrier = pltpu.get_barrier_semaphore()
    i = c // 2

    def plane(k):
        @pl.when(k != c)
        def _():
            pl.semaphore_signal(barrier, inc=1, device_id=(z, k), device_id_type=MESH)

    def column(k):
        @pl.when(k != z)
        def _():
            pl.semaphore_signal(barrier, inc=1, device_id=(k, 2 * i), device_id_type=MESH)
            pl.semaphore_signal(barrier, inc=1, device_id=(k, 2 * i + 1), device_id_type=MESH)

    each(SHARDS, plane)
    each(GROUPS, column)


def greeted():
    pl.semaphore_wait(pltpu.get_barrier_semaphore(), SHARDS - 1 + 2 * (GROUPS - 1))


def one_hot(rows, cols, source):
    o = lax.broadcasted_iota(jnp.int32, (rows, cols), 0)
    n = lax.broadcasted_iota(jnp.int32, (rows, cols), 1)
    return jnp.where(n == source(o), 1.0, 0.0).astype(BF)


def piece_source(o):
    s = o % 32
    r = o // 64
    hh = (o // 32) % 2
    block = jnp.where(s < 16, 16 * hh + s, jnp.where(s < 20, 16 + 4 * hh + s, 20 + 4 * hh + s))
    return jnp.where(s < 24, 8 * block + r, -1)


def kernel(
    seq_ref, inv_ref, vis_ref, len_ref, q, d, kv, img,
    gq, gkv, gimg,
    pieces, z1buf, stage, z2buf, kvp, qi, ta, tb, tm, ds, gather_p, spread_p,
    q2, d2, kvloc, kvimg, kvtxt, imgd,
    bias, ibias, valid, el, dwl, stat, sp, kp, vp, dkl, dvl,
    dq2, dkvloc, dkvimg, dkvtxt, heads,
    rsi, rst, hb0, hb1, hb2, dtx, rows, zb, stage2, tx, kvo,
    z1s, z2s, txs, sws, has, ags, ats, dss, ris, rts, hrs, qrs, xs, y1s, y2s,
    z1r, z2r, tar, tbr, q2r, d2r, klr, kir, ktr, d0r, d1r,
    rir, rtr, h0r, h1r, h2r, gqr, xr, y1r, y2r, lcr,
):
    z = lax.axis_index("rollout")
    c = lax.axis_index("ctx")
    i = c // 2
    h = c % 2
    sib = 2 * i + 1 - h
    scale = 1.0 / math.sqrt(HEAD_DIM)
    to_log2 = scale * math.log2(math.e)
    vis = vis_ref[0]
    nt = (((1,), (1,)), ((), ()))
    greet(z, c)

    blocks = jnp.concatenate([img[:, 128 * k : 128 * (k + 1)].astype(F32) for k in range(48)], axis=0).astype(BF)
    pieces[...] = (
        jnp.dot(one_hot(512, 384, piece_source), blocks, preferred_element_type=F32).astype(BF).reshape(16, 32, 128)
    )
    greeted()

    def z1(j):
        return remote(pieces.at[j], z1buf.at[z], z1s.at[j], z1r, j, c)

    send_all(GROUPS, z, z1, lambda j: pltpu.make_async_copy(pieces.at[j], z1buf.at[z], z1r))

    def text_src(k):
        ii, hh = k // 2, k % 2
        b = ii % 8
        return kv.at[
            b // 4,
            pl.ds(pl.multiple_of(32 * (ii // 8), 32), 32),
            pl.ds(pl.multiple_of(KW * hh + 128 * (b % 4), 128), 128),
        ]

    for place, buf, sem in ((0, ta, tar), (2, tb, tbr)):
        @pl.when(c == place)
        def _():
            send_all(
                SHARDS, c,
                lambda k: remote(text_src(k), buf, txs.at[k], sem, z, k),
                lambda k: pltpu.make_async_copy(text_src(k), buf, sem),
            )

    def cols(core, width):
        return pl.ds(pl.multiple_of(width * core, width), width)

    def rows_of(core, first):
        return pl.ds(pl.multiple_of(first + ROWS * core, 64), ROWS)

    def block(k):
        return pl.ds(pl.multiple_of(16 * k, 16), 16)

    def half_of(k):
        return pl.ds(pl.multiple_of(32 * (k // 8), 32), 32)

    def ahead(n):
        return lax.rem(i + n, CHIPS)

    my_rows = rows_of(h, 0)
    own_rows = rows_of(h, HALO)
    near_rows = rows_of(h, 64)
    swaps = [
        remote(d.at[:, cols(1 - h, QW)], d2.at[my_rows, :], sws.at[0], d2r, z, sib),
        remote(q.at[:, cols(1 - h, QW)], q2.at[my_rows, :], sws.at[1], q2r, z, sib),
        remote(kv.at[:, :, cols(1 - h, KW)], kvloc.at[:, own_rows, :], sws.at[2], klr, z, sib),
    ] + [
        remote(kv.at[:, :, pl.ds(KW * hh, KW)], kvloc.at[:, near_rows, :], has.at[hh], klr, z, 2 * ahead(1) + hh)
        for hh in (0, 1)
    ]
    far = [
        remote(
            kv.at[:, pl.ds(64, 64), pl.ds(KW * hh, KW)], kvloc.at[:, pl.ds(0, 64), :], has.at[2 + hh], klr, z,
            2 * ahead(2) + hh,
        )
        for hh in (0, 1)
    ]
    for copy in swaps:
        copy.start()

    @pl.when(h == 1)
    def _():
        for copy in far:
            copy.start()

    pltpu.make_async_copy(d.at[:, cols(h, QW)], d2.at[my_rows, :], d2r).start()
    pltpu.make_async_copy(q.at[:, cols(h, QW)], q2.at[my_rows, :], q2r).start()
    pltpu.make_async_copy(kv.at[:, :, cols(h, KW)], kvloc.at[:, own_rows, :], klr).start()

    gather_p[...] = one_hot(384, 512, lambda o: (o % 16) * 32 + o // 16)
    spread_p[...] = one_hot(512, 384, lambda o: (o % 32) * 16 + o // 32)

    def slot_positions(lanes):
        r = lax.broadcasted_iota(jnp.int32, (PREFIX, lanes), 0)
        text = r - VIS
        return jnp.where(r < VIS, vis + r, jnp.where(text < vis, text, r))

    pos = CHIP_ROWS * i + lax.broadcasted_iota(jnp.int32, (1, CHIP_ROWS), 1)
    begin = jnp.full((1, CHIP_ROWS), PREFIX, jnp.int32)
    edge = jnp.int32(PREFIX)
    for k in range(16):
        edge = edge + len_ref[0, k]
        begin = jnp.where(pos >= edge, edge, begin)
    begin = jnp.where(pos < PREFIX, pos + 1, begin)
    valid[...] = jnp.where((pos >= vis) & (pos < vis + VIS), 0.0, 1.0)
    bias[:PREFIX, :] = jnp.where(slot_positions(CHIP_ROWS) <= pos, 0.0, NEG)
    at = CHIP_ROWS * i - HALO + lax.broadcasted_iota(jnp.int32, (LOCAL, CHIP_ROWS), 0)
    bias[PREFIX:, :] = jnp.where((at >= begin) & (at <= pos), 0.0, NEG)
    ipos = vis + 16 * i + lax.broadcasted_iota(jnp.int32, (1, 64), 1) % 16
    ibias[...] = jnp.where(slot_positions(64) <= ipos, 0.0, NEG)

    arrived(z1buf, z1r)

    def pick(g):
        stage[g] = z1buf[seq_ref[g]]

    each(GROUPS, pick)
    to_core = z % 2
    slot = 8 * h + z // 2
    here = jnp.where(to_core == h, z, GROUPS)
    here_back = jnp.where(to_core == h, slot, GROUPS)

    def z2(g):
        return remote(stage.at[g], z2buf.at[slot], z2s.at[g], z2r, g, 2 * i + to_core)

    send_all(GROUPS, here, z2, lambda g: pltpu.make_async_copy(stage.at[g], z2buf.at[slot], z2r))

    arrived(ta, tar)
    arrived(tb, tbr)
    t = 32 * (i // 8) + lax.broadcasted_iota(jnp.int32, (32, 128), 0)
    tm[...] = jnp.where(t < vis, ta[...].astype(F32), tb[...].astype(F32)).astype(BF)
    txt_part = kvtxt.at[i % 8, half_of(i), :]

    def atx(k):
        return remote(tm, txt_part, ats.at[k], ktr, z, 2 * k + h)

    send_all(CHIPS, i, atx, lambda k: pltpu.make_async_copy(tm, txt_part, ktr))

    def dsend(k):
        return remote(ds.at[block(k), :], imgd.at[0], dss.at[k], d0r, z, 2 * k + h)

    def dsend1(k):
        return remote(ds.at[block(12 + k), :], imgd.at[1], dss.at[k], d1r, z, 2 * (12 + k) + h)

    arrived(d2, d2r)

    @pl.when(i < 2)
    def _():
        shift = one_hot(VIS, CHIP_ROWS, lambda r: r + vis - CHIP_ROWS * i)
        for part in range(4):
            w = pl.ds(part * 512, 512)
            ds[:, w] = jnp.dot(shift, d2[:, w], preferred_element_type=F32).astype(BF)

    @pl.when(i == 0)
    def _():
        send_all(CHIPS, i, dsend, lambda k: pltpu.make_async_copy(ds.at[block(0), :], imgd.at[0], d0r))

    @pl.when(i == 1)
    def _():
        each(4, lambda k: dsend1(k).start())

    arrived(z2buf, z2r)
    by_head = jnp.dot(gather_p[...], z2buf[...].reshape(512, 128), preferred_element_type=F32).astype(BF)
    by_head = by_head.reshape(24, 16, 128)
    kvp[...] = by_head[16:]

    def aim(k):
        return remote(kvp, kvimg.at[:, block(i), :], ags.at[k], kir, z, 2 * k + h)

    send_all(CHIPS, i, aim, lambda k: pltpu.make_async_copy(kvp, kvimg.at[:, block(i), :], kir))
    qi[...] = by_head[:16]

    arrived(q2, q2r)
    arrived(kvloc, klr)

    def head_cols(e, k):
        return pl.ds(pl.multiple_of(512 * e + 128 * k, 128), 128)

    def key_cols(e):
        return pl.ds(pl.multiple_of(128 * e, 128), 128)

    def local_scores(e):
        k_rows = kvloc[0, :, key_cols(e)]
        v_rows = kvloc[1, :, key_cols(e)]
        for k in range(4):
            w128 = head_cols(e, k)
            n = 4 * e + k
            top = lax.dot_general(k_rows, q2[:, w128], nt, preferred_element_type=F32) * to_log2 + bias[PREFIX:, :]
            peak = jnp.max(top, axis=0, keepdims=True)
            ex = jnp.exp2(top - peak)
            dw = lax.dot_general(v_rows, d2[:, w128], nt, preferred_element_type=F32)
            el[n] = ex
            dwl[n] = dw
            stat[n, 0:1, :] = peak
            stat[n, 1:2, :] = jnp.sum(ex, axis=0, keepdims=True)
            stat[n, 2:3, :] = jnp.sum(ex * dw, axis=0, keepdims=True)

    each(4, local_scores)

    arrived(kvtxt, ktr)
    arrived(imgd.at[0], d0r)

    @pl.when(i >= 12)
    def _():
        arrived(imgd.at[1], d1r)

    arrived(kvimg, kir)

    def rimg(half, k):
        return remote(dkvimg.at[half, :, block(k), :], rsi.at[i, half], ris.at[half, k], rir, z, 2 * k + h)

    def rtxt(k):
        return remote(dkvtxt.at[k % 8, half_of(k), :], rst.at[i], rts.at[k], rtr, z, 2 * k + h)

    def prefix_grads(e):
        kp[:VIS, :] = kvimg[e]
        kp[VIS:, :] = kvtxt[e]
        vp[:VIS, :] = kvimg[4 + e]
        vp[VIS:, :] = kvtxt[4 + e]
        k_rows = kp[...]
        v_rows = vp[...]

        def scores(q_rows, d_rows, mask):
            top = lax.dot_general(k_rows, q_rows, nt, preferred_element_type=F32) * to_log2 + mask
            dw = lax.dot_general(v_rows, d_rows, nt, preferred_element_type=F32)
            return top, jnp.max(top, axis=0, keepdims=True), dw

        q_rows = qi[pl.ds(4 * e, 4)].reshape(64, 128)
        wide = pl.ds(pl.multiple_of(512 * e, 512), 512)
        d_rows = (imgd[0, :, wide].astype(F32) + jnp.where(i >= 12, imgd[1, :, wide].astype(F32), 0.0)).astype(BF)
        d_rows = jnp.concatenate([d_rows[:, 128 * k : 128 * (k + 1)] for k in range(4)], axis=0)
        top, peak, dw = scores(q_rows, d_rows, ibias[...])
        ex = jnp.exp2(top - peak)
        inv = 1.0 / jnp.sum(ex, axis=0, keepdims=True)
        delta = jnp.sum(ex * dw, axis=0, keepdims=True) * inv
        w = ex * inv
        s = (w * (dw - delta)).astype(BF)
        dk = jnp.dot(s, q_rows, preferred_element_type=F32)
        dv = jnp.dot(w.astype(BF), d_rows, preferred_element_type=F32)
        dqi = lax.dot_general(s, k_rows, (((0,), (0,)), ((), ())), preferred_element_type=F32) * scale
        heads[pl.ds(4 * e, 4)] = dqi.astype(BF).reshape(4, 16, 128)

        for k in range(4):
            n = 4 * e + k
            q_rows = q2[:, head_cols(e, k)]
            d_rows = d2[:, head_cols(e, k)]
            top, peak, dw = scores(q_rows, d_rows, bias[:PREFIX, :])
            low = stat[n, 0:1, :]
            peak = jnp.maximum(peak, low)
            ex = jnp.exp2(top - peak)
            shrink = jnp.exp2(low - peak)
            inv = 1.0 / (jnp.sum(ex, axis=0, keepdims=True) + stat[n, 1:2, :] * shrink)
            delta = (jnp.sum(ex * dw, axis=0, keepdims=True) + stat[n, 2:3, :] * shrink) * inv
            inv = inv * valid[...]
            w = ex * inv
            s = (w * (dw - delta)).astype(BF)
            dk = dk + jnp.dot(s, q_rows, preferred_element_type=F32)
            dv = dv + jnp.dot(w.astype(BF), d_rows, preferred_element_type=F32)
            sp[n] = s
            stat[n, 0:1, :] = shrink * inv
            stat[n, 1:2, :] = delta
        dk = (dk * scale).astype(BF)
        dv = dv.astype(BF)
        place = 2 * (e % 2)
        dkvimg[e // 2, place] = dk[:VIS]
        dkvimg[e // 2, place + 1] = dv[:VIS]
        dkvtxt[e] = dk[VIS:]
        dkvtxt[4 + e] = dv[VIS:]

        @pl.when(e % 2 == 1)
        def _():
            half = e // 2
            send_all(
                CHIPS, i,
                lambda k: rimg(half, k),
                lambda k: pltpu.make_async_copy(dkvimg.at[half, :, block(k), :], rsi.at[i, half], rir),
            )

    each(4, prefix_grads)
    send_all(CHIPS, i, rtxt, lambda k: pltpu.make_async_copy(dkvtxt.at[k % 8, half_of(k), :], rst.at[i], rtr))

    def halo_copies(e):
        near, more = 2 * ahead(CHIPS - 1), 2 * ahead(CHIPS - 2)
        return [
            remote(dkvloc.at[e, :, rows_of(s, 64), :], hb1.at[h, e], hrs.at[s, e], h1r, z, near + s) for s in (0, 1)
        ] + [
            remote(dkvloc.at[e, :, pl.ds(0, 64), :], hb2.at[h, e], hrs.at[2, e], h2r, z, more + 1),
            remote(dkvloc.at[e, :, rows_of(1 - h, HALO), :], hb0.at[h, e], hrs.at[3, e], h0r, z, sib),
            remote(dq2.at[e, rows_of(1 - h, 0), :], gq.at[:, out_cols(e)], qrs.at[e], gqr, z, sib),
        ]

    def out_cols(e):
        return pl.ds(pl.multiple_of(QW * h + 512 * e, 512), 512)

    def local_grads(e):
        k_rows = kvloc[0, :, key_cols(e)]
        kt = k_rows.T
        kp[:VIS, :] = kvimg[e]
        kp[VIS:, :] = kvtxt[e]
        kpt = kp[...].T
        for k in range(4):
            n = 4 * e + k
            q_rows = q2[:, head_cols(e, k)]
            d_rows = d2[:, head_cols(e, k)]
            w = el[n] * stat[n, 0:1, :]
            s = (w * (dwl[n] - stat[n, 1:2, :])).astype(BF)
            part = jnp.dot(s, q_rows, preferred_element_type=F32)
            dkl[...] = part if k == 0 else dkl[...] + part
            part = jnp.dot(w.astype(BF), d_rows, preferred_element_type=F32)
            dvl[...] = part if k == 0 else dvl[...] + part
            dqt = jnp.dot(kt, s, preferred_element_type=F32) + jnp.dot(kpt, sp[n], preferred_element_type=F32)
            dq2[e, :, 128 * k : 128 * (k + 1)] = (dqt * scale).T.astype(BF)
        dkvloc[e, 0] = (dkl[...] * scale).astype(BF)
        dkvloc[e, 1] = dvl[...].astype(BF)
        for copy in halo_copies(e):
            copy.start()
        pltpu.make_async_copy(dkvloc.at[e, :, rows_of(h, HALO), :], hb0.at[h, e], h0r).start()
        pltpu.make_async_copy(dq2.at[e, rows_of(h, 0), :], gq.at[:, out_cols(e)], gqr).start()

    def z1_back(r):
        return remote(rows.at[r], zb.at[z], y1s.at[r], y1r, 2 * (r % 8) + h, 2 * i + r // 8)

    txt_slot = dtx.at[h, i % 8, half_of(i), :]

    def reduce_prefix():
        arrived(rsi, rir)
        total = rsi[0].astype(F32)
        for k in range(1, CHIPS):
            total = total + rsi[k].astype(F32)
        total = total.astype(BF)
        for e in range(4):
            for n in range(2):
                heads[16 + 4 * n + e] = total[e // 2, 2 * (e % 2) + n]
        rows[...] = (
            jnp.dot(spread_p[...], heads[...].reshape(384, 128), preferred_element_type=F32)
            .astype(BF)
            .reshape(16, 32, 128)
        )
        send_all(16, here_back, z1_back, lambda r: pltpu.make_async_copy(rows.at[r], zb.at[z], y1r))
        arrived(rst, rtr)
        total = rst[0].astype(F32)
        for k in range(1, CHIPS):
            total = total + rst[k].astype(F32)
        tx[...] = total.astype(BF)
        for n, place in ((0, 0), (1, 2)):
            @pl.when(c != place)
            def _():
                remote(tx, txt_slot, xs.at[n], xr, z, place).start()

            @pl.when(c == place)
            def _():
                pltpu.make_async_copy(tx, txt_slot, xr).start()

    def rest(e):
        local_grads(e)

        @pl.when(e == RS_AT)
        def _():
            reduce_prefix()

    each(4, rest)

    sent_all(GROUPS, z, z1)
    sent_all(GROUPS, here, z2)
    for place, buf, sem in ((0, ta, tar), (2, tb, tbr)):
        @pl.when(c == place)
        def _():
            sent_all(SHARDS, c, lambda k: remote(text_src(k), buf, txs.at[k], sem, z, k))

    for copy in swaps:
        copy.wait_send()

    @pl.when(h == 1)
    def _():
        for copy in far:
            copy.wait_send()

    sent_all(CHIPS, i, atx)
    sent_all(CHIPS, i, aim)

    @pl.when(i == 0)
    def _():
        sent_all(CHIPS, i, dsend)

    @pl.when(i == 1)
    def _():
        each(4, lambda k: dsend1(k).wait_send())

    arrived(zb, y1r)

    def pick_back(g):
        stage2[g] = zb[inv_ref[g]]

    each(GROUPS, pick_back)

    def z2_back(g):
        return remote(stage2.at[g], gimg.at[z], y2s.at[g], y2r, g, c)

    send_all(GROUPS, z, z2_back, lambda g: pltpu.make_async_copy(stage2.at[g], gimg.at[z], y2r))

    for half in (0, 1):
        sent_all(CHIPS, i, lambda k: rimg(half, k))
    sent_all(CHIPS, i, rtxt)
    sent_all(16, here_back, z1_back)
    for n, place in ((0, 0), (1, 2)):
        @pl.when(c != place)
        def _():
            remote(tx, txt_slot, xs.at[n], xr, z, place).wait_send()

    arrived(hb0, h0r)
    arrived(hb1, h1r)

    @pl.when(h == 1)
    def _():
        arrived(hb2, h2r)

    for hh in (0, 1):
        for e in range(4):
            for n in (0, 1):
                w = pl.ds(KW * hh + 128 * e, 128)
                near = hb0[hh, e, n].astype(F32) + hb1[hh, e, n].astype(F32)
                kvo[n, :64, w] = near[:64].astype(BF)
                more = jnp.where(h == 1, hb2[hh, e, n].astype(F32), 0.0)
                kvo[n, 64:, w] = (near[64:] + more).astype(BF)

    t64 = lax.broadcasted_iota(jnp.int32, (PROMPT, 128), 0)
    for place in (0, 2):
        @pl.when(c == place)
        def _():
            arrived(dtx, xr)
            keep = t64 < vis if place == 0 else t64 >= vis
            for hh in (0, 1):
                for b in range(8):
                    kvo[b // 4, :64, pl.ds(KW * hh + 128 * (b % 4), 128)] = jnp.where(
                        keep, dtx[hh, b].astype(F32), 0.0
                    ).astype(BF)

    out = pltpu.make_async_copy(kvo, gkv, lcr)
    out.start()
    each(4, lambda e: [copy.wait_send() for copy in halo_copies(e)] and None)
    arrived(gq, gqr)
    out.wait()
    arrived(gimg, y2r)
    sent_all(GROUPS, z, z2_back)


ANY = pl.BlockSpec(memory_space=pl.ANY)
SMEM = pl.BlockSpec(memory_space=pltpu.SMEM)
DMA = pltpu.SemaphoreType.DMA


def sds(*shape):
    return jax.ShapeDtypeStruct(shape, BF)


def vm(*shape, dtype=BF):
    return pltpu.VMEM(shape, dtype)


def per_device(queries, keys_values, image_rows, cotangent, seq_image, vis_start, comp_lengths):
    groups = jnp.arange(GROUPS, dtype=jnp.int32)
    user = jnp.sum(jnp.where(seq_image[None, :] == groups[:, None], groups[None, :], 0), axis=1, dtype=jnp.int32)
    gq, gkv, gimg = pl.pallas_call(
        kernel,
        out_shape=[sds(ROWS, 2 * QW), sds(2, ROWS, 2 * KW), sds(16, 32, 128)],
        in_specs=[SMEM] * 4 + [ANY] * 3 + [pl.BlockSpec(memory_space=pltpu.VMEM)],
        out_specs=[ANY] * 3,
        scratch_shapes=[
            vm(16, 32, 128), vm(16, 32, 128), vm(16, 32, 128), vm(16, 32, 128), vm(8, 16, 128), vm(16, 16, 128),
            vm(32, 128), vm(32, 128), vm(32, 128), vm(VIS, QW), vm(384, 512), vm(512, 384),
            vm(CHIP_ROWS, QW), vm(CHIP_ROWS, QW), vm(2, LOCAL, KW), vm(8, VIS, 128), vm(8, PROMPT, 128),
            vm(2, 16, QW),
            vm(KEYS, CHIP_ROWS, dtype=F32), vm(PREFIX, 64, dtype=F32), vm(1, CHIP_ROWS, dtype=F32),
            vm(16, LOCAL, CHIP_ROWS, dtype=F32), vm(16, LOCAL, CHIP_ROWS, dtype=F32),
            vm(16, 8, CHIP_ROWS, dtype=F32), vm(16, PREFIX, CHIP_ROWS),
            vm(PREFIX, 128), vm(PREFIX, 128), vm(LOCAL, 128, dtype=F32), vm(LOCAL, 128, dtype=F32),
            vm(4, CHIP_ROWS, 512), vm(4, 2, LOCAL, 128), vm(2, 4, VIS, 128), vm(8, PROMPT, 128), vm(24, 16, 128),
            vm(16, 2, 4, 16, 128), vm(16, 32, 128), vm(2, 4, 2, ROWS, 128), vm(2, 4, 2, ROWS, 128),
            vm(2, 4, 2, 64, 128), vm(2, 8, 64, 128), vm(16, 32, 128), vm(16, 32, 128), vm(16, 32, 128), vm(32, 128),
            vm(2, ROWS, 2 * KW),
            DMA((16,)), DMA((16,)), DMA((32,)), DMA((3,)), DMA((4,)), DMA((16,)), DMA((16,)), DMA((16,)),
            DMA((2, 16)), DMA((16,)), DMA((4, 4)), DMA((4,)), DMA((2,)), DMA((16,)), DMA((16,)),
        ] + [DMA(())] * 21,
        compiler_params=pltpu.CompilerParams(
            collective_id=0, has_side_effects=True, vmem_limit_bytes=56 * 2**20
        ),
        name="grads",
    )(seq_image, user, vis_start, comp_lengths, queries[0], cotangent[0], keys_values[0], image_rows[0])

    gimg = gimg.reshape(8, 2, 32, 128)
    own = jnp.concatenate(
        [
            gimg[:, :, :16].reshape(8, 2 * QW),
            gimg[:, :, 16:20].reshape(8, 2 * KW),
            gimg[:, :, 20:24].reshape(8, 2 * KW),
        ],
        axis=1,
    )
    return (gq[None], gkv[None], own[None])


def solution(mesh):
    placed = (
        P("rollout", "ctx", None),
        P("rollout", None, "ctx", None),
        P("rollout", "ctx", None),
        P("rollout", "ctx", None),
        P(),
        P("rollout"),
        P("rollout", None),
    )
    return jax.shard_map(
        per_device,
        mesh=mesh,
        in_specs=placed,
        out_specs=(
            P("rollout", "ctx", None),
            P("rollout", None, "ctx", None),
            P("rollout", "ctx", None),
        ),
        check_vma=False,
    )
```

time: 120 us -> 96.1 us (0.80)
  Pallas kernels: 109 us -> 89.1 us
  local copies, waits for them, and re-layouts: 8.74 us -> 4.13 us
    pallas_call x3 -> x1, Pallas kernels: 109 us -> 89.1 us  [per_device(): pl.pallas_call(kernel, out_shape=[sds(ROWS, 2 * QW), sds(2, ROWS, 2 * KW)...]
    unnamed x17 -> x9, local copies, waits for them, and re-layouts: 6.96 us -> 3.18 us
    slice x2 -> x0, local copies, waits for them, and re-layouts: 1.59 us -> none  [the longest x1 0.85 us: per_device(): q_part = rows[:, :2 * QW].reshape(8, 2, 16, 128)]
where the time goes in v2:
time: 96.1 us; the launch traced here: 95.9 us
  Pallas kernels  89.1 us (93%)
  local copies, waits for them, and re-layouts  4.13 us (4%)
  between operations  1.36 us (1%)
  other arithmetic  1.28 us (1%)
    pallas_call x1, Pallas kernels, per_device(): pl.pallas_call(kernel, out_shape=[sds(ROWS, 2 * QW), sds(2, ROWS, 2 * KW)...  89.1 us
    unnamed x9, local copies, waits for them, and re-layouts  3.18 us

profile of v2, /device:TPU:1, one launch (start us, length us, event | category | flops | bytes accessed | tf_op | source)
XLA Modules:
  0.0 95.9 jit_solution(4606398592623542279)
XLA Ops:
  0.6 0.0 copy-start.2
  1.3 0.0 copy-done.2
  1.3 0.6 select_reduce_fusion.inv_ref
  1.9 89.1 %grads.1 = (bf16[128,4096]{1,0:T(8,128)(2,1)}, bf16[2,128,1024]{2,1,0:T(8,128)(2,1)}, bf16[16,32,128]{2,1,0:T(8,128)(2,1)}) custom-call(s32[16]{0:T(128)} %seq_ref.1, s32[16]{0:T(128)} %select_reduce_fusion.inv_ref, s32[1]{0:T(128)S(6)} %copy.15.vis_ref, s32[1,16]{1,0:T(1,128)} %len_ref.1, bf16[128,4096]{1,0:T(8,128)(2,1)} %bitcast.14, ...), custom_call_target="tpu_custom_call" | custom-call | tf_op jit(solution)/shard_map/grads/pallas_call | solution.py:581
  91.1 0.0 copy-start.1
  91.1 0.9 fusion
  92.1 0.0 copy-done.1
  92.1 0.6 maximum_bitcast_fusion
  92.8 0.0 copy-start
  92.8 2.3 %copy.16 = bf16[1,128,4096]{2,1,0:T(8,128)(2,1)} copy(bf16[1,128,4096]{2,1,0:T(8,128)(2,1)} %bitcast.16) | data formatting | bytes 2097152
  95.1 0.0 copy-done
  95.1 0.8 copy.17
  (4 shorter events, 0.1 us)
Async XLA Ops:
  0.6 0.7 copy-start.2
  91.1 1.0 %copy-start.1 = (bf16[16,32,128]{2,1,0:T(8,128)(2,1)S(1)}, bf16[16,32,128]{2,1,0:T(8,128)(2,1)}, u32[]{:S(2)}) copy-start(bf16[16,32,128]{2,1,0:T(8,128)(2,1)} %get-tuple-element.8) | copy-start | bytes 393220
  92.8 2.3 %copy-start = (bf16[2,128,1024]{2,1,0:T(8,128)(2,1)S(1)}, bf16[2,128,1024]{2,1,0:T(8,128)(2,1)}, u32[]{:S(2)}) copy-start(bf16[2,128,1024]{2,1,0:T(8,128)(2,1)} %get-tuple-element.7) | copy-start | bytes 1572868

commit v3 on v2

--- a/solution.py
+++ b/solution.py
@@ -28,6 +28,9 @@
 BF = jnp.bfloat16
 F32 = jnp.float32
 NEG = -1e30
+NEAR = 4
+PARTS = 2 * NEAR
+LIMIT = 56
 RS_AT = 2
 
 
@@ -50,6 +53,15 @@
 
 
 def send_all(count, me, copy, local):
+    each(count - 1, lambda k: copy(lax.rem(me + 1 + k, count)).start())
+    local(me).start()
+
+
+def sent_all(count, me, copy):
+    each(count - 1, lambda k: copy(lax.rem(me + 1 + k, count)).wait_send())
+
+
+def send_but(count, me, copy, local):
     def body(k):
         @pl.when(k != me)
         def _():
@@ -62,7 +74,7 @@
     each(count, body)
 
 
-def sent_all(count, me, copy):
+def sent_but(count, me, copy):
     def body(k):
         @pl.when(k != me)
         def _():
@@ -75,23 +87,22 @@
     barrier = pltpu.get_barrier_semaphore()
     i = c // 2
 
+    def column(k):
+        for to in (lax.rem(z + 1 + k, GROUPS), lax.rem(z + GROUPS - 1 - k, GROUPS)):
+            for core in (0, 1):
+                pl.semaphore_signal(barrier, inc=1, device_id=(to, 2 * i + core), device_id_type=MESH)
+
     def plane(k):
-        @pl.when(k != c)
-        def _():
-            pl.semaphore_signal(barrier, inc=1, device_id=(z, k), device_id_type=MESH)
-
-    def column(k):
-        @pl.when(k != z)
-        def _():
-            pl.semaphore_signal(barrier, inc=1, device_id=(k, 2 * i), device_id_type=MESH)
-            pl.semaphore_signal(barrier, inc=1, device_id=(k, 2 * i + 1), device_id_type=MESH)
-
-    each(SHARDS, plane)
-    each(GROUPS, column)
+        pl.semaphore_signal(
+            barrier, inc=1, device_id=(z, lax.rem(c + 1 + k, SHARDS)), device_id_type=MESH
+        )
+
+    each(NEAR, column)
+    each(SHARDS - 1, plane)
 
 
 def greeted():
-    pl.semaphore_wait(pltpu.get_barrier_semaphore(), SHARDS - 1 + 2 * (GROUPS - 1))
+    pl.semaphore_wait(pltpu.get_barrier_semaphore(), SHARDS - 1 + 4 * NEAR)
 
 
 def one_hot(rows, cols, source):
@@ -100,25 +111,44 @@
     return jnp.where(n == source(o), 1.0, 0.0).astype(BF)
 
 
-def piece_source(o):
-    s = o % 32
-    r = o // 64
-    hh = (o // 32) % 2
-    block = jnp.where(s < 16, 16 * hh + s, jnp.where(s < 20, 16 + 4 * hh + s, 20 + 4 * hh + s))
-    return jnp.where(s < 24, 8 * block + r, -1)
+def piece_rows():
+    shape = (8, 48, 384)
+    piece = lax.broadcasted_iota(jnp.int32, shape, 0)
+    y = lax.broadcasted_iota(jnp.int32, shape, 1)
+    n = lax.broadcasted_iota(jnp.int32, shape, 2)
+    half = piece % 2
+    of_kv = y < 16
+    y = jnp.where(of_kv, y, y - 16)
+    row = 2 * (piece // 2) + jnp.where(of_kv, y // 8, y // 16)
+    block = jnp.where(of_kv, 32 + 8 * ((y // 4) % 2) + 4 * half + y % 4, 16 * half + y % 16)
+    return jnp.where(n == 8 * block + row, 1.0, 0.0).astype(BF).reshape(384, 384)
+
+
+def kv_order(o):
+    y = o // 16
+    return (o % 16) * 8 + 4 * (y % 2) + 2 * (y // 4) + (y // 2) % 2
+
+
+def kv_order_back(o):
+    x = o % 8
+    return ((x % 4) // 2 * 4 + x % 2 * 2 + x // 4) * 16 + o // 8
+
+
+def q_order(o):
+    return (o % 16) * 16 + o // 16
 
 
 def kernel(
-    seq_ref, inv_ref, vis_ref, len_ref, q, d, kv, img,
+    seq_ref, vis_ref, len_ref, q, d, kv, img,
     gq, gkv, gimg,
-    pieces, z1buf, stage, z2buf, kvp, qi, ta, tb, tm, ds, gather_p, spread_p,
+    inv_ref, pieces, z1k, z1q, stage, z2k, z2q, kvp, qi, ta, tb, tm, ds, to_rows, kv_p, kv_pb, q_p,
     q2, d2, kvloc, kvimg, kvtxt, imgd,
     bias, ibias, valid, el, dwl, stat, sp, kp, vp, dkl, dvl,
     dq2, dkvloc, dkvimg, dkvtxt, heads,
-    rsi, rst, hb0, hb1, hb2, dtx, rows, zb, stage2, tx, kvo,
+    rsi, rst, hb0, hb1, hb2, dtx, rows, zbk, zbq, stage2, stage3, fin, tx, kvo, io,
     z1s, z2s, txs, sws, has, ags, ats, dss, ris, rts, hrs, qrs, xs, y1s, y2s,
-    z1r, z2r, tar, tbr, q2r, d2r, klr, kir, ktr, d0r, d1r,
-    rir, rtr, h0r, h1r, h2r, gqr, xr, y1r, y2r, lcr,
+    z1r, z2r, kir, y1r, y2r,
+    tar, tbr, q2r, d2r, klr, ktr, d0r, d1r, rir, rtr, h0r, h1r, h2r, gqr, xr, lcr, far_sem,
 ):
     z = lax.axis_index("rollout")
     c = lax.axis_index("ctx")
@@ -132,15 +162,31 @@
     greet(z, c)
 
     blocks = jnp.concatenate([img[:, 128 * k : 128 * (k + 1)].astype(F32) for k in range(48)], axis=0).astype(BF)
-    pieces[...] = (
-        jnp.dot(one_hot(512, 384, piece_source), blocks, preferred_element_type=F32).astype(BF).reshape(16, 32, 128)
-    )
+    in_pieces = piece_rows()
+    pieces[...] = jnp.dot(in_pieces, blocks, preferred_element_type=F32).astype(BF).reshape(8, 48, 128)
     greeted()
-
-    def z1(j):
-        return remote(pieces.at[j], z1buf.at[z], z1s.at[j], z1r, j, c)
-
-    send_all(GROUPS, z, z1, lambda j: pltpu.make_async_copy(pieces.at[j], z1buf.at[z], z1r))
+    for to in (lax.rem(z + NEAR, GROUPS), lax.rem(z + GROUPS - NEAR, GROUPS)):
+        for core in (0, 1):
+            pl.semaphore_signal(far_sem, inc=1, device_id=(to, 2 * i + core), device_id_type=MESH)
+
+    spans = (pl.ds(0, 16), pl.ds(16, 32))
+    z1b, z2b, zbs = (z1k, z1q), (z2k, z2q), (zbk, zbq)
+
+    def z1(p, n):
+        j = lax.rem(z + GROUPS + 1 - NEAR + p, GROUPS)
+        return remote(pieces.at[p // 2 * 2 + j % 2, spans[n]], z1b[n].at[p], z1s.at[n, p], z1r.at[n], j, c)
+
+    def z1_here(n):
+        p = NEAR - 1
+        return pltpu.make_async_copy(
+            pieces.at[p // 2 * 2 + z % 2, spans[n]], z1b[n].at[p], z1r.at[n]
+        )
+
+    others = [p for p in range(PARTS) if p != NEAR - 1]
+    for n in (0, 1):
+        for p in others:
+            z1(p, n).start()
+        z1_here(n).start()
 
     def text_src(k):
         ii, hh = k // 2, k % 2
@@ -205,8 +251,15 @@
     pltpu.make_async_copy(q.at[:, cols(h, QW)], q2.at[my_rows, :], q2r).start()
     pltpu.make_async_copy(kv.at[:, :, cols(h, KW)], kvloc.at[:, own_rows, :], klr).start()
 
-    gather_p[...] = one_hot(384, 512, lambda o: (o % 16) * 32 + o // 16)
-    spread_p[...] = one_hot(512, 384, lambda o: (o % 32) * 16 + o // 32)
+    to_rows[...] = in_pieces.T
+    kv_p[...] = one_hot(128, 128, kv_order)
+    kv_pb[...] = one_hot(128, 128, kv_order_back)
+    q_p[...] = one_hot(256, 256, q_order)
+    for o in range(GROUPS):
+        user = jnp.int32(0)
+        for g in range(GROUPS):
+            user = jnp.where(seq_ref[g] == o, g, user)
+        inv_ref[o] = user
 
     def slot_positions(lanes):
         r = lax.broadcasted_iota(jnp.int32, (PREFIX, lanes), 0)
@@ -227,21 +280,32 @@
     ipos = vis + 16 * i + lax.broadcasted_iota(jnp.int32, (1, 64), 1) % 16
     ibias[...] = jnp.where(slot_positions(64) <= ipos, 0.0, NEG)
 
-    arrived(z1buf, z1r)
-
-    def pick(g):
-        stage[g] = z1buf[seq_ref[g]]
-
-    each(GROUPS, pick)
     to_core = z % 2
     slot = 8 * h + z // 2
     here = jnp.where(to_core == h, z, GROUPS)
     here_back = jnp.where(to_core == h, slot, GROUPS)
 
-    def z2(g):
-        return remote(stage.at[g], z2buf.at[slot], z2s.at[g], z2r, g, 2 * i + to_core)
-
-    send_all(GROUPS, here, z2, lambda g: pltpu.make_async_copy(stage.at[g], z2buf.at[slot], z2r))
+    def part_of(o, j):
+        return jnp.minimum((j - o + NEAR - 1) & (GROUPS - 1), PARTS - 1)
+
+    def z2(g, n):
+        return remote(
+            stage.at[g, spans[n]], z2b[n].at[slot], z2s.at[n, g], z2r.at[n], g, 2 * i + to_core
+        )
+
+    def z2_here(g, n):
+        return pltpu.make_async_copy(stage.at[g, spans[n]], z2b[n].at[slot], z2r.at[n])
+
+    for n in (0, 1):
+        arrived(z1b[n], z1r.at[n])
+
+        def pick(g):
+            stage[g, spans[n]] = z1b[n][part_of(seq_ref[g], z)]
+
+        each(GROUPS, pick)
+        if n == 0:
+            pl.semaphore_wait(far_sem, 4)
+        send_but(GROUPS, here, lambda g: z2(g, n), lambda g: z2_here(g, n))
 
     arrived(ta, tar)
     arrived(tb, tbr)
@@ -277,16 +341,27 @@
     def _():
         each(4, lambda k: dsend1(k).start())
 
-    arrived(z2buf, z2r)
-    by_head = jnp.dot(gather_p[...], z2buf[...].reshape(512, 128), preferred_element_type=F32).astype(BF)
-    by_head = by_head.reshape(24, 16, 128)
-    kvp[...] = by_head[16:]
-
-    def aim(k):
-        return remote(kvp, kvimg.at[:, block(i), :], ags.at[k], kir, z, 2 * k + h)
-
-    send_all(CHIPS, i, aim, lambda k: pltpu.make_async_copy(kvp, kvimg.at[:, block(i), :], kir))
-    qi[...] = by_head[:16]
+    image = seq_ref[z]
+
+    def slot_of(s, rp):
+        even = (image + 1 - NEAR + 2 * rp) & (GROUPS - 1)
+        j = jnp.where((even & 1) == h, even, (even + 1) & (GROUPS - 1))
+        return 8 * s + j // 2
+
+    def come(n):
+        return jnp.concatenate([z2b[n][slot_of(s, rp)] for s in (0, 1) for rp in range(4)], axis=0)
+
+    arrived(z2b[0], z2r.at[0])
+    kvp[...] = jnp.dot(kv_p[...], come(0), preferred_element_type=F32).astype(BF).reshape(2, 4, 16, 128)
+
+    def aim(half, k):
+        return remote(kvp.at[half], kvimg.at[half, :, block(i), :], ags.at[half, k], kir.at[half], z, 2 * k + h)
+
+    for half in (0, 1):
+        send_all(
+            CHIPS, i, lambda k: aim(half, k),
+            lambda k: pltpu.make_async_copy(kvp.at[half], kvimg.at[half, :, block(i), :], kir.at[half]),
+        )
 
     arrived(q2, q2r)
     arrived(kvloc, klr)
@@ -309,12 +384,15 @@
             dw = lax.dot_general(v_rows, d2[:, w128], nt, preferred_element_type=F32)
             el[n] = ex
             dwl[n] = dw
-            stat[n, 0:1, :] = peak
-            stat[n, 1:2, :] = jnp.sum(ex, axis=0, keepdims=True)
-            stat[n, 2:3, :] = jnp.sum(ex * dw, axis=0, keepdims=True)
+            lanes = pl.ds(CHIP_ROWS * k, CHIP_ROWS)
+            stat[e, 0:1, lanes] = peak
+            stat[e, 1:2, lanes] = jnp.sum(ex, axis=0, keepdims=True)
+            stat[e, 2:3, lanes] = jnp.sum(ex * dw, axis=0, keepdims=True)
 
     each(4, local_scores)
 
+    arrived(z2b[1], z2r.at[1])
+    qi[...] = jnp.dot(q_p[...], come(1), preferred_element_type=F32).astype(BF).reshape(16, 16, 128)
     arrived(kvtxt, ktr)
     arrived(imgd.at[0], d0r)
 
@@ -322,18 +400,25 @@
     def _():
         arrived(imgd.at[1], d1r)
 
-    arrived(kvimg, kir)
-
     def rimg(half, k):
         return remote(dkvimg.at[half, :, block(k), :], rsi.at[i, half], ris.at[half, k], rir, z, 2 * k + h)
 
     def rtxt(k):
         return remote(dkvtxt.at[k % 8, half_of(k), :], rst.at[i], rts.at[k], rtr, z, 2 * k + h)
 
+    def four(x):
+        return jnp.concatenate([x] * 4, axis=1)
+
     def prefix_grads(e):
-        kp[:VIS, :] = kvimg[e]
+        place = 2 * (e % 2)
+
+        @pl.when(e % 2 == 0)
+        def _():
+            arrived(kvimg.at[e // 2], kir.at[e // 2])
+
+        kp[:VIS, :] = kvimg[e // 2, place]
         kp[VIS:, :] = kvtxt[e]
-        vp[:VIS, :] = kvimg[4 + e]
+        vp[:VIS, :] = kvimg[e // 2, place + 1]
         vp[VIS:, :] = kvtxt[4 + e]
         k_rows = kp[...]
         v_rows = vp[...]
@@ -358,28 +443,25 @@
         dqi = lax.dot_general(s, k_rows, (((0,), (0,)), ((), ())), preferred_element_type=F32) * scale
         heads[pl.ds(4 * e, 4)] = dqi.astype(BF).reshape(4, 16, 128)
 
-        for k in range(4):
-            n = 4 * e + k
-            q_rows = q2[:, head_cols(e, k)]
-            d_rows = d2[:, head_cols(e, k)]
-            top, peak, dw = scores(q_rows, d_rows, bias[:PREFIX, :])
-            low = stat[n, 0:1, :]
-            peak = jnp.maximum(peak, low)
-            ex = jnp.exp2(top - peak)
-            shrink = jnp.exp2(low - peak)
-            inv = 1.0 / (jnp.sum(ex, axis=0, keepdims=True) + stat[n, 1:2, :] * shrink)
-            delta = (jnp.sum(ex * dw, axis=0, keepdims=True) + stat[n, 2:3, :] * shrink) * inv
-            inv = inv * valid[...]
-            w = ex * inv
-            s = (w * (dw - delta)).astype(BF)
-            dk = dk + jnp.dot(s, q_rows, preferred_element_type=F32)
-            dv = dv + jnp.dot(w.astype(BF), d_rows, preferred_element_type=F32)
-            sp[n] = s
-            stat[n, 0:1, :] = shrink * inv
-            stat[n, 1:2, :] = delta
+        q_rows = jnp.concatenate([q2[:, head_cols(e, k)] for k in range(4)], axis=0)
+        d_rows = jnp.concatenate([d2[:, head_cols(e, k)] for k in range(4)], axis=0)
+        top, peak, dw = scores(q_rows, d_rows, four(bias[:PREFIX, :]))
+        low = stat[e, 0:1, :]
+        peak = jnp.maximum(peak, low)
+        ex = jnp.exp2(top - peak)
+        shrink = jnp.exp2(low - peak)
+        inv = 1.0 / (jnp.sum(ex, axis=0, keepdims=True) + stat[e, 1:2, :] * shrink)
+        delta = (jnp.sum(ex * dw, axis=0, keepdims=True) + stat[e, 2:3, :] * shrink) * inv
+        inv = inv * four(valid[...])
+        w = ex * inv
+        s = (w * (dw - delta)).astype(BF)
+        dk = dk + jnp.dot(s, q_rows, preferred_element_type=F32)
+        dv = dv + jnp.dot(w.astype(BF), d_rows, preferred_element_type=F32)
+        sp[e] = s
+        stat[e, 0:1, :] = shrink * inv
+        stat[e, 1:2, :] = delta
         dk = (dk * scale).astype(BF)
         dv = dv.astype(BF)
-        place = 2 * (e % 2)
         dkvimg[e // 2, place] = dk[:VIS]
         dkvimg[e // 2, place + 1] = dv[:VIS]
         dkvtxt[e] = dk[VIS:]
@@ -394,7 +476,45 @@
                 lambda k: pltpu.make_async_copy(dkvimg.at[half, :, block(k), :], rsi.at[i, half], rir),
             )
 
+    def z1_back(t, n):
+        return remote(
+            stage2.at[t, spans[n]], zbs[n].at[z], y1s.at[n, t], y1r.at[n], 2 * (t % 8) + h, 2 * i + t // 8
+        )
+
+    def back_to_rows(n, value):
+        rows[:, spans[n]] = value.astype(BF).reshape(8, 16 * (n + 1), 128)
+
+        def pick(t):
+            stage2[t, spans[n]] = rows[4 * (t // 8) + part_of(image, 2 * (t % 8) + h) // 2, spans[n]]
+
+        each(16, pick)
+        send_but(
+            16, here_back, lambda t: z1_back(t, n),
+            lambda t: pltpu.make_async_copy(stage2.at[t, spans[n]], zbs[n].at[z], y1r.at[n]),
+        )
+
+    def z2_back(p, n):
+        o = lax.rem(z + GROUPS + NEAR - 1 - p, GROUPS)
+        return remote(
+            stage3.at[p, spans[n]], fin.at[p // 2 * 2 + z % 2, spans[n]], y2s.at[n, p], y2r.at[n], o, c
+        )
+
+    def second_back(n):
+        arrived(zbs[n], y1r.at[n])
+
+        def pick(p):
+            stage3[p, spans[n]] = zbs[n][inv_ref[lax.rem(z + GROUPS + NEAR - 1 - p, GROUPS)]]
+
+        each(PARTS, pick)
+        for p in others:
+            z2_back(p, n).start()
+        p = NEAR - 1
+        pltpu.make_async_copy(
+            stage3.at[p, spans[n]], fin.at[p // 2 * 2 + z % 2, spans[n]], y2r.at[n]
+        ).start()
+
     each(4, prefix_grads)
+    back_to_rows(1, jnp.dot(q_p[...], heads[...].reshape(256, 128), preferred_element_type=F32))
     send_all(CHIPS, i, rtxt, lambda k: pltpu.make_async_copy(dkvtxt.at[k % 8, half_of(k), :], rst.at[i], rtr))
 
     def halo_copies(e):
@@ -413,20 +533,21 @@
     def local_grads(e):
         k_rows = kvloc[0, :, key_cols(e)]
         kt = k_rows.T
-        kp[:VIS, :] = kvimg[e]
+        kp[:VIS, :] = kvimg[e // 2, 2 * (e % 2)]
         kp[VIS:, :] = kvtxt[e]
         kpt = kp[...].T
         for k in range(4):
             n = 4 * e + k
             q_rows = q2[:, head_cols(e, k)]
             d_rows = d2[:, head_cols(e, k)]
-            w = el[n] * stat[n, 0:1, :]
-            s = (w * (dwl[n] - stat[n, 1:2, :])).astype(BF)
+            lanes = pl.ds(CHIP_ROWS * k, CHIP_ROWS)
+            w = el[n] * stat[e, 0:1, lanes]
+            s = (w * (dwl[n] - stat[e, 1:2, lanes])).astype(BF)
             part = jnp.dot(s, q_rows, preferred_element_type=F32)
             dkl[...] = part if k == 0 else dkl[...] + part
             part = jnp.dot(w.astype(BF), d_rows, preferred_element_type=F32)
             dvl[...] = part if k == 0 else dvl[...] + part
-            dqt = jnp.dot(kt, s, preferred_element_type=F32) + jnp.dot(kpt, sp[n], preferred_element_type=F32)
+            dqt = jnp.dot(kt, s, preferred_element_type=F32) + jnp.dot(kpt, sp[e, :, lanes], preferred_element_type=F32)
             dq2[e, :, 128 * k : 128 * (k + 1)] = (dqt * scale).T.astype(BF)
         dkvloc[e, 0] = (dkl[...] * scale).astype(BF)
         dkvloc[e, 1] = dvl[...].astype(BF)
@@ -435,9 +556,6 @@
         pltpu.make_async_copy(dkvloc.at[e, :, rows_of(h, HALO), :], hb0.at[h, e], h0r).start()
         pltpu.make_async_copy(dq2.at[e, rows_of(h, 0), :], gq.at[:, out_cols(e)], gqr).start()
 
-    def z1_back(r):
-        return remote(rows.at[r], zb.at[z], y1s.at[r], y1r, 2 * (r % 8) + h, 2 * i + r // 8)
-
     txt_slot = dtx.at[h, i % 8, half_of(i), :]
 
     def reduce_prefix():
@@ -445,16 +563,8 @@
         total = rsi[0].astype(F32)
         for k in range(1, CHIPS):
             total = total + rsi[k].astype(F32)
-        total = total.astype(BF)
-        for e in range(4):
-            for n in range(2):
-                heads[16 + 4 * n + e] = total[e // 2, 2 * (e % 2) + n]
-        rows[...] = (
-            jnp.dot(spread_p[...], heads[...].reshape(384, 128), preferred_element_type=F32)
-            .astype(BF)
-            .reshape(16, 32, 128)
-        )
-        send_all(16, here_back, z1_back, lambda r: pltpu.make_async_copy(rows.at[r], zb.at[z], y1r))
+        total = total.astype(BF).reshape(128, 128)
+        back_to_rows(0, jnp.dot(kv_pb[...], total, preferred_element_type=F32))
         arrived(rst, rtr)
         total = rst[0].astype(F32)
         for k in range(1, CHIPS):
@@ -478,8 +588,12 @@
 
     each(4, rest)
 
-    sent_all(GROUPS, z, z1)
-    sent_all(GROUPS, here, z2)
+    second_back(1)
+
+    for n in (0, 1):
+        for p in others:
+            z1(p, n).wait_send()
+        sent_but(GROUPS, here, lambda g: z2(g, n))
     for place, buf, sem in ((0, ta, tar), (2, tb, tbr)):
         @pl.when(c == place)
         def _():
@@ -494,7 +608,8 @@
             copy.wait_send()
 
     sent_all(CHIPS, i, atx)
-    sent_all(CHIPS, i, aim)
+    for half in (0, 1):
+        sent_all(CHIPS, i, lambda k: aim(half, k))
 
     @pl.when(i == 0)
     def _():
@@ -504,22 +619,13 @@
     def _():
         each(4, lambda k: dsend1(k).wait_send())
 
-    arrived(zb, y1r)
-
-    def pick_back(g):
-        stage2[g] = zb[inv_ref[g]]
-
-    each(GROUPS, pick_back)
-
-    def z2_back(g):
-        return remote(stage2.at[g], gimg.at[z], y2s.at[g], y2r, g, c)
-
-    send_all(GROUPS, z, z2_back, lambda g: pltpu.make_async_copy(stage2.at[g], gimg.at[z], y2r))
+    second_back(0)
 
     for half in (0, 1):
         sent_all(CHIPS, i, lambda k: rimg(half, k))
     sent_all(CHIPS, i, rtxt)
-    sent_all(16, here_back, z1_back)
+    for n in (0, 1):
+        sent_but(16, here_back, lambda t: z1_back(t, n))
     for n, place in ((0, 0), (1, 2)):
         @pl.when(c != place)
         def _():
@@ -558,11 +664,21 @@
     each(4, lambda e: [copy.wait_send() for copy in halo_copies(e)] and None)
     arrived(gq, gqr)
     out.wait()
-    arrived(gimg, y2r)
-    sent_all(GROUPS, z, z2_back)
+    for n in (0, 1):
+        arrived(fin.at[:, spans[n]], y2r.at[n])
+    blocks = jnp.dot(to_rows[...], fin[...].reshape(384, 128), preferred_element_type=F32)
+    for k in range(48):
+        io[:, 128 * k : 128 * (k + 1)] = blocks[8 * k : 8 * (k + 1)].astype(BF)
+    out = pltpu.make_async_copy(io, gimg, lcr)
+    out.start()
+    for n in (0, 1):
+        for p in others:
+            z2_back(p, n).wait_send()
+    out.wait()
 
 
 ANY = pl.BlockSpec(memory_space=pl.ANY)
+HBM = pl.BlockSpec(memory_space=pltpu.HBM)
 SMEM = pl.BlockSpec(memory_space=pltpu.SMEM)
 DMA = pltpu.SemaphoreType.DMA
 
@@ -576,45 +692,36 @@
 
 
 def per_device(queries, keys_values, image_rows, cotangent, seq_image, vis_start, comp_lengths):
-    groups = jnp.arange(GROUPS, dtype=jnp.int32)
-    user = jnp.sum(jnp.where(seq_image[None, :] == groups[:, None], groups[None, :], 0), axis=1, dtype=jnp.int32)
     gq, gkv, gimg = pl.pallas_call(
         kernel,
-        out_shape=[sds(ROWS, 2 * QW), sds(2, ROWS, 2 * KW), sds(16, 32, 128)],
-        in_specs=[SMEM] * 4 + [ANY] * 3 + [pl.BlockSpec(memory_space=pltpu.VMEM)],
+        out_shape=[sds(ROWS, 2 * QW), sds(2, ROWS, 2 * KW), sds(8, 2 * QW + 4 * KW)],
+        in_specs=[SMEM] * 3 + [HBM] * 3 + [pl.BlockSpec(memory_space=pltpu.VMEM)],
         out_specs=[ANY] * 3,
         scratch_shapes=[
-            vm(16, 32, 128), vm(16, 32, 128), vm(16, 32, 128), vm(16, 32, 128), vm(8, 16, 128), vm(16, 16, 128),
-            vm(32, 128), vm(32, 128), vm(32, 128), vm(VIS, QW), vm(384, 512), vm(512, 384),
-            vm(CHIP_ROWS, QW), vm(CHIP_ROWS, QW), vm(2, LOCAL, KW), vm(8, VIS, 128), vm(8, PROMPT, 128),
+            pltpu.SMEM((16,), jnp.int32),
+            vm(8, 48, 128), vm(8, 16, 128), vm(8, 32, 128), vm(16, 48, 128), vm(16, 16, 128), vm(16, 32, 128),
+            vm(2, 4, 16, 128), vm(16, 16, 128),
+            vm(32, 128), vm(32, 128), vm(32, 128), vm(VIS, QW), vm(384, 384), vm(128, 128), vm(128, 128), vm(256, 256),
+            vm(CHIP_ROWS, QW), vm(CHIP_ROWS, QW), vm(2, LOCAL, KW), vm(2, 4, VIS, 128), vm(8, PROMPT, 128),
             vm(2, 16, QW),
             vm(KEYS, CHIP_ROWS, dtype=F32), vm(PREFIX, 64, dtype=F32), vm(1, CHIP_ROWS, dtype=F32),
             vm(16, LOCAL, CHIP_ROWS, dtype=F32), vm(16, LOCAL, CHIP_ROWS, dtype=F32),
-            vm(16, 8, CHIP_ROWS, dtype=F32), vm(16, PREFIX, CHIP_ROWS),
+            vm(4, 8, 4 * CHIP_ROWS, dtype=F32), vm(4, PREFIX, 4 * CHIP_ROWS),
             vm(PREFIX, 128), vm(PREFIX, 128), vm(LOCAL, 128, dtype=F32), vm(LOCAL, 128, dtype=F32),
-            vm(4, CHIP_ROWS, 512), vm(4, 2, LOCAL, 128), vm(2, 4, VIS, 128), vm(8, PROMPT, 128), vm(24, 16, 128),
+            vm(4, CHIP_ROWS, 512), vm(4, 2, LOCAL, 128), vm(2, 4, VIS, 128), vm(8, PROMPT, 128), vm(16, 16, 128),
             vm(16, 2, 4, 16, 128), vm(16, 32, 128), vm(2, 4, 2, ROWS, 128), vm(2, 4, 2, ROWS, 128),
-            vm(2, 4, 2, 64, 128), vm(2, 8, 64, 128), vm(16, 32, 128), vm(16, 32, 128), vm(16, 32, 128), vm(32, 128),
-            vm(2, ROWS, 2 * KW),
-            DMA((16,)), DMA((16,)), DMA((32,)), DMA((3,)), DMA((4,)), DMA((16,)), DMA((16,)), DMA((16,)),
-            DMA((2, 16)), DMA((16,)), DMA((4, 4)), DMA((4,)), DMA((2,)), DMA((16,)), DMA((16,)),
-        ] + [DMA(())] * 21,
+            vm(2, 4, 2, 64, 128), vm(2, 8, 64, 128), vm(8, 48, 128), vm(16, 16, 128), vm(16, 32, 128),
+            vm(16, 48, 128), vm(8, 48, 128), vm(8, 48, 128), vm(32, 128), vm(2, ROWS, 2 * KW), vm(8, 2 * QW + 4 * KW),
+            DMA((2, 8)), DMA((2, 16)), DMA((32,)), DMA((3,)), DMA((4,)), DMA((2, 16)), DMA((16,)), DMA((16,)),
+            DMA((2, 16)), DMA((16,)), DMA((4, 4)), DMA((4,)), DMA((2,)), DMA((2, 16)), DMA((2, 8)),
+            DMA((2,)), DMA((2,)), DMA((2,)), DMA((2,)), DMA((2,)),
+        ] + [DMA(())] * 16 + [pltpu.SemaphoreType.REGULAR],
         compiler_params=pltpu.CompilerParams(
-            collective_id=0, has_side_effects=True, vmem_limit_bytes=56 * 2**20
+            collective_id=0, has_side_effects=True, vmem_limit_bytes=LIMIT * 2**20
         ),
         name="grads",
-    )(seq_image, user, vis_start, comp_lengths, queries[0], cotangent[0], keys_values[0], image_rows[0])
-
-    gimg = gimg.reshape(8, 2, 32, 128)
-    own = jnp.concatenate(
-        [
-            gimg[:, :, :16].reshape(8, 2 * QW),
-            gimg[:, :, 16:20].reshape(8, 2 * KW),
-            gimg[:, :, 20:24].reshape(8, 2 * KW),
-        ],
-        axis=1,
-    )
-    return (gq[None], gkv[None], own[None])
+    )(seq_image, vis_start, comp_lengths, queries[0], cotangent[0], keys_values[0], image_rows[0])
+    return (gq[None], gkv[None], gimg[None])
 
 
 def solution(mesh):

time: 96.1 us -> 83.8 us (0.87)
  Pallas kernels: 89.1 us -> 78.3 us
  other arithmetic: 1.28 us -> 0 us
    pallas_call x1, Pallas kernels: 89.1 us -> 78.3 us  [per_device(): pl.pallas_call(kernel, out_shape=[sds(ROWS, 2 * QW), sds(2, ROWS, 2 * KW)...]
    unnamed x9 -> x7, local copies, waits for them, and re-layouts: 3.18 us -> 3.95 us
where the time goes in v3:
time: 83.8 us; the launch traced here: 83.5 us
  Pallas kernels  78.3 us (93%)
  local copies, waits for them, and re-layouts  3.95 us (5%)
  between operations  1.3 us (2%)
    pallas_call x1, Pallas kernels, per_device(): pl.pallas_call(kernel, out_shape=[sds(ROWS, 2 * QW), sds(2, ROWS, 2 * KW)...  78.3 us
    unnamed x7, local copies, waits for them, and re-layouts  3.95 us

profile of v3, /device:TPU:1, one launch (start us, length us, event | category | flops | bytes accessed | tf_op | source)
XLA Modules:
  0.0 83.5 jit_solution(800151192188702960)
XLA Ops:
  1.3 78.3 %grads.1 = (bf16[128,4096]{1,0:T(8,128)(2,1)}, bf16[2,128,1024]{2,1,0:T(8,128)(2,1)}, bf16[8,6144]{1,0:T(8,128)(2,1)}) custom-call(s32[16]{0:T(128)} %seq_ref.1, s32[1]{0:T(128)S(6)} %copy.13.vis_ref, s32[1,16]{1,0:T(1,128)} %len_ref.1, bf16[128,4096]{1,0:T(8,128)(2,1)} %bitcast.7, bf16[128,4096]{1,0:T(8,128)(2,1)} %bitcast.8, ...), custom_call_target="tpu_custom_call" | custom-call | tf_op jit(solution)/shard_map/grads/pallas_call | solution.py:695
  79.6 0.0 copy-start
  79.6 2.3 %copy.14 = bf16[1,128,4096]{2,1,0:T(8,128)(2,1)} copy(bf16[1,128,4096]{2,1,0:T(8,128)(2,1)} %bitcast.9) | data formatting | bytes 2097152
  81.9 0.0 copy-done
  81.9 0.0 copy-start.1
  81.9 0.8 copy.15
  82.7 0.2 copy-done.1
  82.9 0.6 copy.16
Async XLA Ops:
  79.6 2.4 %copy-start = (bf16[2,128,1024]{2,1,0:T(8,128)(2,1)S(1)}, bf16[2,128,1024]{2,1,0:T(8,128)(2,1)}, u32[]{:S(2)}) copy-start(bf16[2,128,1024]{2,1,0:T(8,128)(2,1)} %get-tuple-element.7) | copy-start | bytes 1572868
  81.9 1.0 %copy-start.1 = (bf16[8,6144]{1,0:T(8,128)(2,1)S(1)}, bf16[8,6144]{1,0:T(8,128)(2,1)}, u32[]{:S(2)}) copy-start(bf16[8,6144]{1,0:T(8,128)(2,1)} %get-tuple-element.8) | copy-start | bytes 294916

commit v4 on v3

--- a/solution.py
+++ b/solution.py
@@ -30,7 +30,7 @@
 NEG = -1e30
 NEAR = 4
 PARTS = 2 * NEAR
-LIMIT = 56
+LIMIT = 40
 RS_AT = 2
 
 
@@ -121,7 +121,7 @@
     y = jnp.where(of_kv, y, y - 16)
     row = 2 * (piece // 2) + jnp.where(of_kv, y // 8, y // 16)
     block = jnp.where(of_kv, 32 + 8 * ((y // 4) % 2) + 4 * half + y % 4, 16 * half + y % 16)
-    return jnp.where(n == 8 * block + row, 1.0, 0.0).astype(BF).reshape(384, 384)
+    return jnp.where(n == 8 * block + row, 1.0, 0.0)
 
 
 def kv_order(o):
@@ -141,14 +141,14 @@
 def kernel(
     seq_ref, vis_ref, len_ref, q, d, kv, img,
     gq, gkv, gimg,
-    inv_ref, pieces, z1k, z1q, stage, z2k, z2q, kvp, qi, ta, tb, tm, ds, to_rows, kv_p, kv_pb, q_p,
+    inv_ref, pieces, z1k, z1q, stage, z2k, z2q, kvp, qi, ta, tb, tm, ds, dnext, to_kv, to_q, kv_p, kv_pb, q_p,
     q2, d2, kvloc, kvimg, kvtxt, imgd,
     bias, ibias, valid, el, dwl, stat, sp, kp, vp, dkl, dvl,
     dq2, dkvloc, dkvimg, dkvtxt, heads,
     rsi, rst, hb0, hb1, hb2, dtx, rows, zbk, zbq, stage2, stage3, fin, tx, kvo, io,
-    z1s, z2s, txs, sws, has, ags, ats, dss, ris, rts, hrs, qrs, xs, y1s, y2s,
-    z1r, z2r, kir, y1r, y2r,
-    tar, tbr, q2r, d2r, klr, ktr, d0r, d1r, rir, rtr, h0r, h1r, h2r, gqr, xr, lcr, far_sem,
+    z1s, z2s, txs, sws, has, ags, ats, dss, dns, ris, rts, hrs, qrs, xs, y1s, y2s, ims,
+    z1r, z2r, kir, y1r, y2r, klr, kfr,
+    tar, tbr, q2r, d2r, ktr, d0r, dnr, rir, rtr, h0r, h1r, h2r, gqr, xr, lcr, far_sem,
 ):
     z = lax.axis_index("rollout")
     c = lax.axis_index("ctx")
@@ -159,11 +159,14 @@
     to_log2 = scale * math.log2(math.e)
     vis = vis_ref[0]
     nt = (((1,), (1,)), ((), ()))
+    load = pltpu.make_async_copy(img, io, lcr)
+    load.start()
     greet(z, c)
 
-    blocks = jnp.concatenate([img[:, 128 * k : 128 * (k + 1)].astype(F32) for k in range(48)], axis=0).astype(BF)
     in_pieces = piece_rows()
-    pieces[...] = jnp.dot(in_pieces, blocks, preferred_element_type=F32).astype(BF).reshape(8, 48, 128)
+    load.wait()
+    blocks = jnp.concatenate([io[:, 128 * k : 128 * (k + 1)].astype(F32) for k in range(48)], axis=0).astype(BF)
+    pieces[...] = jnp.dot(in_pieces.astype(BF).reshape(384, 384), blocks, preferred_element_type=F32).astype(BF).reshape(8, 48, 128)
     greeted()
     for to in (lax.rem(z + NEAR, GROUPS), lax.rem(z + GROUPS - NEAR, GROUPS)):
         for core in (0, 1):
@@ -224,34 +227,103 @@
     my_rows = rows_of(h, 0)
     own_rows = rows_of(h, HALO)
     near_rows = rows_of(h, 64)
+
+    def kv_cols(core, e):
+        return pl.ds(pl.multiple_of(KW * core + 128 * e, 128), 128)
+
+    sends_near = (i >= 1) & (i < CHIPS - 1)
+    sends_far = (i >= 2) & (i < CHIPS - 1)
+    has_near = i >= 2
+    has_far = i >= 3
+    far_rows = pl.ds(0, 64)
+
+    def own_in(e):
+        return remote(
+            kv.at[:, :, kv_cols(1 - h, e)], kvloc.at[e, :, own_rows, :], has.at[2, e], klr.at[e], z, sib
+        )
+
+    def near_in(e):
+        return [
+            remote(
+                kv.at[:, :, kv_cols(hh, e)], kvloc.at[e, :, near_rows, :], has.at[hh, e], klr.at[e], z,
+                2 * ahead(1) + hh,
+            )
+            for hh in (0, 1)
+        ]
+
+    def far_in(e):
+        return remote(
+            kvloc.at[e, :, pl.ds(HALO - 64, 64), :], kvloc.at[e, :, far_rows, :], has.at[3, e], kfr.at[e], z,
+            2 * ahead(1) + h,
+        )
+
+    def halo_start(e):
+        @pl.when(sends_near)
+        def _():
+            for copy in near_in(e):
+                copy.start()
+
+        own_in(e).start()
+        pltpu.make_async_copy(kv.at[:, :, kv_cols(h, e)], kvloc.at[e, :, own_rows, :], klr.at[e]).start()
+
+    def near_come(e):
+        @pl.when(has_near)
+        def _():
+            arrived(kvloc.at[e, :, pl.ds(64, LOCAL - 64), :], klr.at[e])
+
+        @pl.when(i < 2)
+        def _():
+            arrived(kvloc.at[e, :, pl.ds(HALO, CHIP_ROWS), :], klr.at[e])
+            kvloc[e, :, 64:HALO, :] = jnp.zeros((2, HALO - 64, 128), BF)
+
+        @pl.when(sends_far)
+        def _():
+            far_in(e).start()
+
+    def far_come(e):
+        @pl.when(has_far)
+        def _():
+            arrived(kvloc.at[e, :, far_rows, :], kfr.at[e])
+
+        @pl.when(i < 3)
+        def _():
+            kvloc[e, :, 0:64, :] = jnp.zeros((2, 64, 128), BF)
+
     swaps = [
         remote(d.at[:, cols(1 - h, QW)], d2.at[my_rows, :], sws.at[0], d2r, z, sib),
         remote(q.at[:, cols(1 - h, QW)], q2.at[my_rows, :], sws.at[1], q2r, z, sib),
-        remote(kv.at[:, :, cols(1 - h, KW)], kvloc.at[:, own_rows, :], sws.at[2], klr, z, sib),
-    ] + [
-        remote(kv.at[:, :, pl.ds(KW * hh, KW)], kvloc.at[:, near_rows, :], has.at[hh], klr, z, 2 * ahead(1) + hh)
-        for hh in (0, 1)
     ]
-    far = [
-        remote(
-            kv.at[:, pl.ds(64, 64), pl.ds(KW * hh, KW)], kvloc.at[:, pl.ds(0, 64), :], has.at[2 + hh], klr, z,
-            2 * ahead(2) + hh,
-        )
-        for hh in (0, 1)
-    ]
+    halo_start(0)
     for copy in swaps:
         copy.start()
-
-    @pl.when(h == 1)
-    def _():
-        for copy in far:
-            copy.start()
-
     pltpu.make_async_copy(d.at[:, cols(h, QW)], d2.at[my_rows, :], d2r).start()
     pltpu.make_async_copy(q.at[:, cols(h, QW)], q2.at[my_rows, :], q2r).start()
-    pltpu.make_async_copy(kv.at[:, :, cols(h, KW)], kvloc.at[:, own_rows, :], klr).start()
-
-    to_rows[...] = in_pieces.T
+    halo_start(1)
+
+    def dnear(hh):
+        return remote(d.at[pl.ds(0, 64), pl.ds(QW * hh, QW)], dnext, dns.at[hh], dnr, z, hh)
+
+    def dsend(k):
+        return remote(ds.at[block(k), :], imgd, dss.at[k], d0r, z, 2 * k + h)
+
+    @pl.when(c == 2)
+    def _():
+        for hh in (0, 1):
+            dnear(hh).start()
+
+    def rest_of_image():
+        arrived(dnext, dnr)
+        shift = one_hot(64, CHIP_ROWS, lambda r: r + 192 + vis)
+        more = one_hot(64, 64, lambda r: r + 192 + vis - CHIP_ROWS)
+        for part in range(4):
+            w = pl.ds(part * 512, 512)
+            rows_d = jnp.dot(shift, d2[:, w], preferred_element_type=F32)
+            rows_d = rows_d + jnp.dot(more, dnext[:, w], preferred_element_type=F32)
+            ds[192:, w] = rows_d.astype(BF)
+        each(4, lambda k: dsend(k + 12).start())
+
+    to_kv[...] = in_pieces[:, :16, 256:].astype(BF).reshape(128, 128).T
+    to_q[...] = in_pieces[:, 16:, :256].astype(BF).reshape(256, 256).T
     kv_p[...] = one_hot(128, 128, kv_order)
     kv_pb[...] = one_hot(128, 128, kv_order_back)
     q_p[...] = one_hot(256, 256, q_order)
@@ -307,39 +379,18 @@
             pl.semaphore_wait(far_sem, 4)
         send_but(GROUPS, here, lambda g: z2(g, n), lambda g: z2_here(g, n))
 
-    arrived(ta, tar)
-    arrived(tb, tbr)
-    t = 32 * (i // 8) + lax.broadcasted_iota(jnp.int32, (32, 128), 0)
-    tm[...] = jnp.where(t < vis, ta[...].astype(F32), tb[...].astype(F32)).astype(BF)
-    txt_part = kvtxt.at[i % 8, half_of(i), :]
-
-    def atx(k):
-        return remote(tm, txt_part, ats.at[k], ktr, z, 2 * k + h)
-
-    send_all(CHIPS, i, atx, lambda k: pltpu.make_async_copy(tm, txt_part, ktr))
-
-    def dsend(k):
-        return remote(ds.at[block(k), :], imgd.at[0], dss.at[k], d0r, z, 2 * k + h)
-
-    def dsend1(k):
-        return remote(ds.at[block(12 + k), :], imgd.at[1], dss.at[k], d1r, z, 2 * (12 + k) + h)
-
-    arrived(d2, d2r)
-
-    @pl.when(i < 2)
+    @pl.when(i == 0)
     def _():
-        shift = one_hot(VIS, CHIP_ROWS, lambda r: r + vis - CHIP_ROWS * i)
+        arrived(d2, d2r)
+        shift = one_hot(192, CHIP_ROWS, lambda r: r + vis)
         for part in range(4):
             w = pl.ds(part * 512, 512)
-            ds[:, w] = jnp.dot(shift, d2[:, w], preferred_element_type=F32).astype(BF)
-
-    @pl.when(i == 0)
-    def _():
-        send_all(CHIPS, i, dsend, lambda k: pltpu.make_async_copy(ds.at[block(0), :], imgd.at[0], d0r))
-
-    @pl.when(i == 1)
-    def _():
-        each(4, lambda k: dsend1(k).start())
+            ds[:192, w] = jnp.dot(shift, d2[:, w], preferred_element_type=F32).astype(BF)
+        pltpu.make_async_copy(ds.at[block(0), :], imgd, d0r).start()
+        each(11, lambda k: dsend(k + 1).start())
+
+    halo_start(2)
+    halo_start(3)
 
     image = seq_ref[z]
 
@@ -351,30 +402,33 @@
     def come(n):
         return jnp.concatenate([z2b[n][slot_of(s, rp)] for s in (0, 1) for rp in range(4)], axis=0)
 
-    arrived(z2b[0], z2r.at[0])
-    kvp[...] = jnp.dot(kv_p[...], come(0), preferred_element_type=F32).astype(BF).reshape(2, 4, 16, 128)
-
     def aim(half, k):
         return remote(kvp.at[half], kvimg.at[half, :, block(i), :], ags.at[half, k], kir.at[half], z, 2 * k + h)
 
-    for half in (0, 1):
-        send_all(
-            CHIPS, i, lambda k: aim(half, k),
-            lambda k: pltpu.make_async_copy(kvp.at[half], kvimg.at[half, :, block(i), :], kir.at[half]),
-        )
+    def hand_round():
+        arrived(z2b[0], z2r.at[0])
+        kvp[...] = jnp.dot(kv_p[...], come(0), preferred_element_type=F32).astype(BF).reshape(2, 4, 16, 128)
+
+        for half in (0, 1):
+            send_all(
+                CHIPS, i, lambda k: aim(half, k),
+                lambda k: pltpu.make_async_copy(kvp.at[half], kvimg.at[half, :, block(i), :], kir.at[half]),
+            )
 
     arrived(q2, q2r)
-    arrived(kvloc, klr)
+
+    @pl.when(i > 0)
+    def _():
+        arrived(d2, d2r)
+
 
     def head_cols(e, k):
         return pl.ds(pl.multiple_of(512 * e + 128 * k, 128), 128)
 
-    def key_cols(e):
-        return pl.ds(pl.multiple_of(128 * e, 128), 128)
-
     def local_scores(e):
-        k_rows = kvloc[0, :, key_cols(e)]
-        v_rows = kvloc[1, :, key_cols(e)]
+        far_come(e)
+        k_rows = kvloc[e, 0]
+        v_rows = kvloc[e, 1]
         for k in range(4):
             w128 = head_cols(e, k)
             n = 4 * e + k
@@ -389,16 +443,11 @@
             stat[e, 1:2, lanes] = jnp.sum(ex, axis=0, keepdims=True)
             stat[e, 2:3, lanes] = jnp.sum(ex * dw, axis=0, keepdims=True)
 
-    each(4, local_scores)
-
-    arrived(z2b[1], z2r.at[1])
-    qi[...] = jnp.dot(q_p[...], come(1), preferred_element_type=F32).astype(BF).reshape(16, 16, 128)
-    arrived(kvtxt, ktr)
-    arrived(imgd.at[0], d0r)
-
-    @pl.when(i >= 12)
-    def _():
-        arrived(imgd.at[1], d1r)
+    def prefix_come():
+        arrived(z2b[1], z2r.at[1])
+        qi[...] = jnp.dot(q_p[...], come(1), preferred_element_type=F32).astype(BF).reshape(16, 16, 128)
+        arrived(kvtxt, ktr)
+        arrived(imgd, d0r)
 
     def rimg(half, k):
         return remote(dkvimg.at[half, :, block(k), :], rsi.at[i, half], ris.at[half, k], rir, z, 2 * k + h)
@@ -411,6 +460,10 @@
 
     def prefix_grads(e):
         place = 2 * (e % 2)
+
+        @pl.when(e == 0)
+        def _():
+            prefix_come()
 
         @pl.when(e % 2 == 0)
         def _():
@@ -430,7 +483,7 @@
 
         q_rows = qi[pl.ds(4 * e, 4)].reshape(64, 128)
         wide = pl.ds(pl.multiple_of(512 * e, 512), 512)
-        d_rows = (imgd[0, :, wide].astype(F32) + jnp.where(i >= 12, imgd[1, :, wide].astype(F32), 0.0)).astype(BF)
+        d_rows = imgd[:, wide]
         d_rows = jnp.concatenate([d_rows[:, 128 * k : 128 * (k + 1)] for k in range(4)], axis=0)
         top, peak, dw = scores(q_rows, d_rows, ibias[...])
         ex = jnp.exp2(top - peak)
@@ -513,25 +566,98 @@
             stage3.at[p, spans[n]], fin.at[p // 2 * 2 + z % 2, spans[n]], y2r.at[n]
         ).start()
 
-    each(4, prefix_grads)
+    near_come(0)
+
+    @pl.when(i == 0)
+    def _():
+        rest_of_image()
+
+    hand_round()
+
+    arrived(ta, tar)
+    arrived(tb, tbr)
+    t = 32 * (i // 8) + lax.broadcasted_iota(jnp.int32, (32, 128), 0)
+    tm[...] = jnp.where(t < vis, ta[...].astype(F32), tb[...].astype(F32)).astype(BF)
+    txt_part = kvtxt.at[i % 8, half_of(i), :]
+
+    def atx(k):
+        return remote(tm, txt_part, ats.at[k], ktr, z, 2 * k + h)
+
+    send_all(CHIPS, i, atx, lambda k: pltpu.make_async_copy(tm, txt_part, ktr))
+    near_come(1)
+
+    def step(n):
+        @pl.when((n != 2) & (n < 4))
+        def _():
+            local_scores(n)
+
+        @pl.when(n == 1)
+        def _():
+            near_come(2)
+            near_come(3)
+
+        @pl.when(n > 0)
+        def _():
+            prefix_grads(n - 1)
+
+        @pl.when(n == 2)
+        def _():
+            local_scores(n)
+
+    each(5, step)
     back_to_rows(1, jnp.dot(q_p[...], heads[...].reshape(256, 128), preferred_element_type=F32))
     send_all(CHIPS, i, rtxt, lambda k: pltpu.make_async_copy(dkvtxt.at[k % 8, half_of(k), :], rst.at[i], rtr))
 
-    def halo_copies(e):
-        near, more = 2 * ahead(CHIPS - 1), 2 * ahead(CHIPS - 2)
+    def near_back(e):
         return [
-            remote(dkvloc.at[e, :, rows_of(s, 64), :], hb1.at[h, e], hrs.at[s, e], h1r, z, near + s) for s in (0, 1)
-        ] + [
-            remote(dkvloc.at[e, :, pl.ds(0, 64), :], hb2.at[h, e], hrs.at[2, e], h2r, z, more + 1),
+            remote(
+                dkvloc.at[e, :, rows_of(s, 64), :], hb1.at[h, e], hrs.at[s, e], h1r, z, 2 * ahead(CHIPS - 1) + s
+            )
+            for s in (0, 1)
+        ]
+
+    def far_back(e):
+        return remote(
+            dkvloc.at[e, :, far_rows, :], hb2.at[h, e], hrs.at[2, e], h2r, z, 2 * ahead(CHIPS - 2) + 1
+        )
+
+    def own_back(e):
+        return [
             remote(dkvloc.at[e, :, rows_of(1 - h, HALO), :], hb0.at[h, e], hrs.at[3, e], h0r, z, sib),
             remote(dq2.at[e, rows_of(1 - h, 0), :], gq.at[:, out_cols(e)], qrs.at[e], gqr, z, sib),
         ]
 
+    def back_start(e):
+        @pl.when(has_near)
+        def _():
+            for copy in near_back(e):
+                copy.start()
+
+        @pl.when(has_far)
+        def _():
+            far_back(e).start()
+
+        for copy in own_back(e):
+            copy.start()
+
+    def back_left(e):
+        @pl.when(has_near)
+        def _():
+            for copy in near_back(e):
+                copy.wait_send()
+
+        @pl.when(has_far)
+        def _():
+            far_back(e).wait_send()
+
+        for copy in own_back(e):
+            copy.wait_send()
+
     def out_cols(e):
         return pl.ds(pl.multiple_of(QW * h + 512 * e, 512), 512)
 
     def local_grads(e):
-        k_rows = kvloc[0, :, key_cols(e)]
+        k_rows = kvloc[e, 0]
         kt = k_rows.T
         kp[:VIS, :] = kvimg[e // 2, 2 * (e % 2)]
         kp[VIS:, :] = kvtxt[e]
@@ -551,8 +677,7 @@
             dq2[e, :, 128 * k : 128 * (k + 1)] = (dqt * scale).T.astype(BF)
         dkvloc[e, 0] = (dkl[...] * scale).astype(BF)
         dkvloc[e, 1] = dvl[...].astype(BF)
-        for copy in halo_copies(e):
-            copy.start()
+        back_start(e)
         pltpu.make_async_copy(dkvloc.at[e, :, rows_of(h, HALO), :], hb0.at[h, e], h0r).start()
         pltpu.make_async_copy(dq2.at[e, rows_of(h, 0), :], gq.at[:, out_cols(e)], gqr).start()
 
@@ -602,10 +727,19 @@
     for copy in swaps:
         copy.wait_send()
 
-    @pl.when(h == 1)
-    def _():
-        for copy in far:
-            copy.wait_send()
+    def halo_left(e):
+        own_in(e).wait_send()
+
+        @pl.when(sends_near)
+        def _():
+            for copy in near_in(e):
+                copy.wait_send()
+
+        @pl.when(sends_far)
+        def _():
+            far_in(e).wait_send()
+
+    each(4, halo_left)
 
     sent_all(CHIPS, i, atx)
     for half in (0, 1):
@@ -613,13 +747,27 @@
 
     @pl.when(i == 0)
     def _():
-        sent_all(CHIPS, i, dsend)
-
-    @pl.when(i == 1)
+        each(15, lambda k: dsend(k + 1).wait_send())
+
+    @pl.when(c == 2)
     def _():
-        each(4, lambda k: dsend1(k).wait_send())
+        for hh in (0, 1):
+            dnear(hh).wait_send()
 
     second_back(0)
+
+    def assemble(n, order):
+        blocks = jnp.dot(order[...], fin[:, spans[n]].reshape(-1, 128), preferred_element_type=F32)
+        begin, width = ((2 * QW, 4 * KW), (0, 2 * QW))[n]
+        for k in range(width // 128):
+            io[:, begin + 128 * k : begin + 128 * (k + 1)] = blocks[8 * k : 8 * (k + 1)].astype(BF)
+        span = pl.ds(begin, width)
+        copy = pltpu.make_async_copy(io.at[:, span], gimg.at[:, span], ims.at[n])
+        copy.start()
+        return copy
+
+    arrived(fin.at[:, spans[1]], y2r.at[1])
+    first = assemble(1, to_q)
 
     for half in (0, 1):
         sent_all(CHIPS, i, lambda k: rimg(half, k))
@@ -632,9 +780,13 @@
             remote(tx, txt_slot, xs.at[n], xr, z, place).wait_send()
 
     arrived(hb0, h0r)
-    arrived(hb1, h1r)
-
-    @pl.when(h == 1)
+    @pl.when(sends_near)
+    def _():
+        arrived(hb1, h1r)
+
+    gives_far = (h == 1) & (i >= 1) & (i < CHIPS - 2)
+
+    @pl.when(gives_far)
     def _():
         arrived(hb2, h2r)
 
@@ -642,9 +794,9 @@
         for e in range(4):
             for n in (0, 1):
                 w = pl.ds(KW * hh + 128 * e, 128)
-                near = hb0[hh, e, n].astype(F32) + hb1[hh, e, n].astype(F32)
+                near = hb0[hh, e, n].astype(F32) + jnp.where(sends_near, hb1[hh, e, n].astype(F32), 0.0)
                 kvo[n, :64, w] = near[:64].astype(BF)
-                more = jnp.where(h == 1, hb2[hh, e, n].astype(F32), 0.0)
+                more = jnp.where(gives_far, hb2[hh, e, n].astype(F32), 0.0)
                 kvo[n, 64:, w] = (near[64:] + more).astype(BF)
 
     t64 = lax.broadcasted_iota(jnp.int32, (PROMPT, 128), 0)
@@ -661,24 +813,19 @@
 
     out = pltpu.make_async_copy(kvo, gkv, lcr)
     out.start()
-    each(4, lambda e: [copy.wait_send() for copy in halo_copies(e)] and None)
+    each(4, back_left)
     arrived(gq, gqr)
     out.wait()
-    for n in (0, 1):
-        arrived(fin.at[:, spans[n]], y2r.at[n])
-    blocks = jnp.dot(to_rows[...], fin[...].reshape(384, 128), preferred_element_type=F32)
-    for k in range(48):
-        io[:, 128 * k : 128 * (k + 1)] = blocks[8 * k : 8 * (k + 1)].astype(BF)
-    out = pltpu.make_async_copy(io, gimg, lcr)
-    out.start()
+    arrived(fin.at[:, spans[0]], y2r.at[0])
+    last = assemble(0, to_kv)
     for n in (0, 1):
         for p in others:
             z2_back(p, n).wait_send()
-    out.wait()
+    first.wait()
+    last.wait()
 
 
 ANY = pl.BlockSpec(memory_space=pl.ANY)
-HBM = pl.BlockSpec(memory_space=pltpu.HBM)
 SMEM = pl.BlockSpec(memory_space=pltpu.SMEM)
 DMA = pltpu.SemaphoreType.DMA
 
@@ -695,15 +842,16 @@
     gq, gkv, gimg = pl.pallas_call(
         kernel,
         out_shape=[sds(ROWS, 2 * QW), sds(2, ROWS, 2 * KW), sds(8, 2 * QW + 4 * KW)],
-        in_specs=[SMEM] * 3 + [HBM] * 3 + [pl.BlockSpec(memory_space=pltpu.VMEM)],
+        in_specs=[SMEM] * 3 + [ANY] * 4,
         out_specs=[ANY] * 3,
         scratch_shapes=[
             pltpu.SMEM((16,), jnp.int32),
             vm(8, 48, 128), vm(8, 16, 128), vm(8, 32, 128), vm(16, 48, 128), vm(16, 16, 128), vm(16, 32, 128),
             vm(2, 4, 16, 128), vm(16, 16, 128),
-            vm(32, 128), vm(32, 128), vm(32, 128), vm(VIS, QW), vm(384, 384), vm(128, 128), vm(128, 128), vm(256, 256),
-            vm(CHIP_ROWS, QW), vm(CHIP_ROWS, QW), vm(2, LOCAL, KW), vm(2, 4, VIS, 128), vm(8, PROMPT, 128),
-            vm(2, 16, QW),
+            vm(32, 128), vm(32, 128), vm(32, 128), vm(VIS, QW), vm(64, QW), vm(128, 128), vm(256, 256),
+            vm(128, 128), vm(128, 128), vm(256, 256),
+            vm(CHIP_ROWS, QW), vm(CHIP_ROWS, QW), vm(4, 2, LOCAL, 128), vm(2, 4, VIS, 128), vm(8, PROMPT, 128),
+            vm(16, QW),
             vm(KEYS, CHIP_ROWS, dtype=F32), vm(PREFIX, 64, dtype=F32), vm(1, CHIP_ROWS, dtype=F32),
             vm(16, LOCAL, CHIP_ROWS, dtype=F32), vm(16, LOCAL, CHIP_ROWS, dtype=F32),
             vm(4, 8, 4 * CHIP_ROWS, dtype=F32), vm(4, PREFIX, 4 * CHIP_ROWS),
@@ -712,15 +860,19 @@
             vm(16, 2, 4, 16, 128), vm(16, 32, 128), vm(2, 4, 2, ROWS, 128), vm(2, 4, 2, ROWS, 128),
             vm(2, 4, 2, 64, 128), vm(2, 8, 64, 128), vm(8, 48, 128), vm(16, 16, 128), vm(16, 32, 128),
             vm(16, 48, 128), vm(8, 48, 128), vm(8, 48, 128), vm(32, 128), vm(2, ROWS, 2 * KW), vm(8, 2 * QW + 4 * KW),
-            DMA((2, 8)), DMA((2, 16)), DMA((32,)), DMA((3,)), DMA((4,)), DMA((2, 16)), DMA((16,)), DMA((16,)),
+            DMA((2, 8)), DMA((2, 16)), DMA((32,)), DMA((2,)), DMA((4, 4)), DMA((2, 16)), DMA((16,)), DMA((16,)), DMA((2,)),
             DMA((2, 16)), DMA((16,)), DMA((4, 4)), DMA((4,)), DMA((2,)), DMA((2, 16)), DMA((2, 8)),
-            DMA((2,)), DMA((2,)), DMA((2,)), DMA((2,)), DMA((2,)),
-        ] + [DMA(())] * 16 + [pltpu.SemaphoreType.REGULAR],
+            DMA((2,)),
+            DMA((2,)), DMA((2,)), DMA((2,)), DMA((2,)), DMA((2,)), DMA((4,)), DMA((4,)),
+        ] + [DMA(())] * 15 + [pltpu.SemaphoreType.REGULAR],
         compiler_params=pltpu.CompilerParams(
             collective_id=0, has_side_effects=True, vmem_limit_bytes=LIMIT * 2**20
         ),
         name="grads",
-    )(seq_image, vis_start, comp_lengths, queries[0], cotangent[0], keys_values[0], image_rows[0])
+    )(
+        seq_image, vis_start, comp_lengths,
+        *(pltpu.with_memory_space_constraint(x[0], pltpu.HBM) for x in (queries, cotangent, keys_values, image_rows)),
+    )
     return (gq[None], gkv[None], gimg[None])
 
 

time: 83.8 us -> 79.5 us (0.949)
  Pallas kernels: 78.3 us -> 75 us
  local copies, waits for them, and re-layouts: 3.95 us -> 3.06 us
    pallas_call x1, Pallas kernels: 78.3 us -> 75 us  [per_device(): pl.pallas_call(kernel, out_shape=[sds(ROWS, 2 * QW), sds(2, ROWS, 2 * KW)...]
    unnamed x7, local copies, waits for them, and re-layouts: 3.95 us -> 3.06 us
where the time goes in v4:
time: 79.5 us; the launch traced here: 79.3 us
  Pallas kernels  75 us (94%)
  local copies, waits for them, and re-layouts  3.06 us (4%)
  between operations  1.3 us (2%)
    pallas_call x1, Pallas kernels, per_device(): pl.pallas_call(kernel, out_shape=[sds(ROWS, 2 * QW), sds(2, ROWS, 2 * KW)...  75 us
    unnamed x7, local copies, waits for them, and re-layouts  3.06 us

profile of v4, /device:TPU:1, one launch (start us, length us, event | category | flops | bytes accessed | tf_op | source)
XLA Modules:
  0.0 79.3 jit_solution(5731488547139492504)
XLA Ops:
  1.3 0.0 copy-start
  1.3 0.0 copy-start.1
  1.3 0.6 copy-done
  1.9 0.0 copy-done.1
  2.0 75.0 %grads.1 = (bf16[128,4096]{1,0:T(8,128)(2,1)S(1)}, bf16[2,128,1024]{2,1,0:T(8,128)(2,1)S(1)}, bf16[8,6144]{1,0:T(8,128)(2,1)S(1)}) custom-call(s32[16]{0:T(128)S(1)} %copy-done, s32[1]{0:T(128)S(6)} %copy.13.vis_ref, s32[1,16]{1,0:T(1,128)S(1)} %copy-done.1, bf16[128,4096]{1,0:T(8,128)(2,1)} %bitcast.10, bf16[128,4096]{1,0:T(8,128)(2,1)} %bitcast.11, ...), custom_call_target="tpu_custom_call" | custom-call | tf_op jit(solution)/shard_map/grads/pallas_call | solution.py:842
  76.9 1.0 %copy.14 = bf16[1,128,4096]{2,1,0:T(8,128)(2,1)} copy(bf16[1,128,4096]{2,1,0:T(8,128)(2,1)S(1)} %bitcast.7) | data formatting | bytes 2097152
  77.9 0.8 copy.15
  78.7 0.6 copy.16
Async XLA Ops:
  1.3 0.7 copy-start
  1.3 0.7 copy-start.1

commit v5 on v4

--- a/solution.py
+++ b/solution.py
@@ -870,7 +870,8 @@
         ),
         name="grads",
     )(
-        seq_image, vis_start, comp_lengths,
+        pltpu.with_memory_space_constraint(seq_image, pltpu.HBM), vis_start,
+        pltpu.with_memory_space_constraint(comp_lengths, pltpu.HBM),
         *(pltpu.with_memory_space_constraint(x[0], pltpu.HBM) for x in (queries, cotangent, keys_values, image_rows)),
     )
     return (gq[None], gkv[None], gimg[None])

time: 79.5 us -> 79 us (level)
    unnamed x7 -> x3, local copies, waits for them, and re-layouts: 3.06 us -> 2.41 us
where the time goes in v5:
time: 79 us; the launch traced here: 78.8 us
  Pallas kernels  75.1 us (95%)
  local copies, waits for them, and re-layouts  2.41 us (3%)
  between operations  1.29 us (2%)
    pallas_call x1, Pallas kernels, per_device(): pl.pallas_call(kernel, out_shape=[sds(ROWS, 2 * QW), sds(2, ROWS, 2 * KW)...  75.1 us
    unnamed x3, local copies, waits for them, and re-layouts  2.41 us

profile of v5, /device:TPU:1, one launch (start us, length us, event | category | flops | bytes accessed | tf_op | source)
XLA Modules:
  0.0 78.8 jit_solution(6699992521818831653)
XLA Ops:
  1.3 75.1 %grads.1 = (bf16[128,4096]{1,0:T(8,128)(2,1)S(1)}, bf16[2,128,1024]{2,1,0:T(8,128)(2,1)S(1)}, bf16[8,6144]{1,0:T(8,128)(2,1)S(1)}) custom-call(s32[16]{0:T(128)} %seq_ref.1, s32[1]{0:T(128)S(6)} %copy.13.vis_ref, s32[1,16]{1,0:T(1,128)} %len_ref.1, bf16[128,4096]{1,0:T(8,128)(2,1)} %bitcast.10, bf16[128,4096]{1,0:T(8,128)(2,1)} %bitcast.11, ...), custom_call_target="tpu_custom_call" | custom-call | tf_op jit(solution)/shard_map/grads/pallas_call | solution.py:842
  76.4 1.0 %copy.14 = bf16[1,128,4096]{2,1,0:T(8,128)(2,1)} copy(bf16[1,128,4096]{2,1,0:T(8,128)(2,1)S(1)} %bitcast.7) | data formatting | bytes 2097152
  77.4 0.8 %copy.15 = bf16[1,2,128,1024]{3,2,1,0:T(8,128)(2,1)} copy(bf16[1,2,128,1024]{3,2,1,0:T(8,128)(2,1)S(1)} %bitcast.8) | data formatting | bytes 1048576
  78.2 0.6 copy.16

commit v6 on v5

--- a/solution.py
+++ b/solution.py
@@ -816,13 +816,12 @@
     each(4, back_left)
     arrived(gq, gqr)
     out.wait()
-    arrived(fin.at[:, spans[0]], y2r.at[0])
-    last = assemble(0, to_kv)
     for n in (0, 1):
         for p in others:
             z2_back(p, n).wait_send()
     first.wait()
-    last.wait()
+    arrived(fin.at[:, spans[0]], y2r.at[0])
+    assemble(0, to_kv).wait()
 
 
 ANY = pl.BlockSpec(memory_space=pl.ANY)

time: 79 us -> 79 us (level)
  no operation moved by 1% of the time
where the time goes in v6:
time: 79 us; the launch traced here: 78.8 us
  Pallas kernels  75.1 us (95%)
  local copies, waits for them, and re-layouts  2.41 us (3%)
  between operations  1.29 us (2%)
    pallas_call x1, Pallas kernels, per_device(): pl.pallas_call(kernel, out_shape=[sds(ROWS, 2 * QW), sds(2, ROWS, 2 * KW)...  75.1 us
    unnamed x3, local copies, waits for them, and re-layouts  2.41 us

profile of v6, /device:TPU:1, one launch (start us, length us, event | category | flops | bytes accessed | tf_op | source)
XLA Modules:
  0.0 78.8 jit_solution(544163740600123500)
XLA Ops:
  1.3 75.1 %grads.1 = (bf16[128,4096]{1,0:T(8,128)(2,1)S(1)}, bf16[2,128,1024]{2,1,0:T(8,128)(2,1)S(1)}, bf16[8,6144]{1,0:T(8,128)(2,1)S(1)}) custom-call(s32[16]{0:T(128)} %seq_ref.1, s32[1]{0:T(128)S(6)} %copy.13.vis_ref, s32[1,16]{1,0:T(1,128)} %len_ref.1, bf16[128,4096]{1,0:T(8,128)(2,1)} %bitcast.10, bf16[128,4096]{1,0:T(8,128)(2,1)} %bitcast.11, ...), custom_call_target="tpu_custom_call" | custom-call | tf_op jit(solution)/shard_map/grads/pallas_call | solution.py:841
  76.4 1.0 %copy.14 = bf16[1,128,4096]{2,1,0:T(8,128)(2,1)} copy(bf16[1,128,4096]{2,1,0:T(8,128)(2,1)S(1)} %bitcast.7) | data formatting | bytes 2097152
  77.4 0.8 %copy.15 = bf16[1,2,128,1024]{3,2,1,0:T(8,128)(2,1)} copy(bf16[1,2,128,1024]{3,2,1,0:T(8,128)(2,1)S(1)} %bitcast.8) | data formatting | bytes 1048576
  78.2 0.6 copy.16
